TPU v7x, 128 devices: a whole 4x4x4 slice. The times are simulated.
128 devices in a mesh: feat: 4 (over y), seed: 32 (over z, x, core).
Axes of the slice: x: 4, y: 4, z: 4, core: 2. Of those that a mesh axis runs over, the one named last changes fastest.
Arguments:
- node_feats: bfloat16 [131072, 768], P('seed', 'feat'), may hold values from -12 to 12
- seed_feats: bfloat16 [768, 32768], P('feat', 'seed'), may hold values from -6 to 6
- w_self: bfloat16 [768, 1024], P('feat'), may hold values from -0.21875 to 0.21875
- w_neigh: bfloat16 [768, 1024], P('feat'), may hold values from -0.21875 to 0.21875
- bias: float32 [1024], replicated, may hold values from -3 to 3
- send_list: int32 [32, 32, 256], P('seed'), may hold values from 0 to 4095
- nbr_slot: int32 [32768, 25], P('seed'), may hold values from 0 to 8191, as said below
- cotangent: bfloat16 [32768, 1024], P('seed', 'feat'), may hold values from -0.13183594 to 0.13183594
Outputs:
- hidden: bfloat16 [32768, 1024], P('seed', 'feat')
- grad_self: float32 [768, 1024], P('feat')
- grad_neigh: float32 [768, 1024], P('feat')
- grad_bias: float32 [1024], replicated
Inputs may be any that keep to these rules, and one draw needn't show every extreme that they name: `nbr_slot`: slots may repeat; slot t names entry t % 256 of what partition t // 256 addresses to the seed's block.
All inputs are finite; a program needn't handle non-finite values.
Results may differ from a plain program's by a relative error of at most 0.003.
Values may be sent and summed in bfloat16 or wider, within the bound.
A program may use at most 448 MiB of HBM per device.

v0:
```python
import jax
import jax.numpy as jnp
from jax import lax
from jax.sharding import PartitionSpec as P


def silu_slope(values):
    logistic = jax.nn.sigmoid(values)
    return logistic * (1.0 + values * (1.0 - logistic))


def local(node_feats, seed_feats, w_self, w_neigh, bias, send_list, nbr_slot, cotangent):
    seed_rows, fanout = nbr_slot.shape
    col_share = cotangent.shape[1]
    slot_rows = send_list.shape[1] * send_list.shape[2]
    flat_slot = nbr_slot.reshape(-1)
    owners = jnp.repeat(jnp.arange(seed_rows, dtype=jnp.int32), fanout)
    counts = (
        jnp.zeros((seed_rows, slot_rows), jnp.float32)
        .at[owners, flat_slot]
        .add(1.0)
        .astype(jnp.bfloat16)
    )
    picked = jnp.take(node_feats, send_list.reshape(-1), axis=0)
    self_term = jnp.einsum("fs,fh->sh", seed_feats, w_self, preferred_element_type=jnp.float32)
    arrived = lax.all_to_all(picked, "seed", split_axis=0, concat_axis=0, tiled=True)
    averaged = jnp.dot(counts, arrived, preferred_element_type=jnp.float32) / fanout
    neigh_term = jnp.dot(averaged, w_neigh.astype(jnp.float32), precision=lax.Precision.HIGHEST)
    partial_value = self_term + neigh_term
    col_start = lax.axis_index("feat") * col_share
    bias_share = lax.dynamic_slice_in_dim(bias, col_start, col_share, 0)
    pre_share = (
        lax.psum_scatter(partial_value, "feat", scatter_dimension=1, tiled=True) + bias_share
    )
    hidden = jax.nn.silu(pre_share).astype(jnp.bfloat16)
    grad_share = (cotangent.astype(jnp.float32) * silu_slope(pre_share)).astype(jnp.bfloat16)
    grad_pre = lax.all_gather(grad_share, "feat", axis=1, tiled=True)
    grad_bias = jnp.sum(grad_pre.astype(jnp.float32), axis=0)
    grad_self = jnp.einsum("fs,sh->fh", seed_feats, grad_pre, preferred_element_type=jnp.float32)
    grad_neigh = jnp.einsum(
        "sf,sh->fh",
        averaged,
        grad_pre.astype(jnp.float32),
        precision=lax.Precision.HIGHEST,
        preferred_element_type=jnp.float32,
    )
    grad_self, grad_neigh, grad_bias = lax.psum((grad_self, grad_neigh, grad_bias), "seed")
    return (hidden, grad_self, grad_neigh, grad_bias)


def solution(mesh):
    placed = (
        P("seed", "feat"),
        P("feat", "seed"),
        P("feat", None),
        P("feat", None),
        P(),
        P("seed", None, None),
        P("seed", None),
        P("seed", "feat"),
    )
    return jax.shard_map(
        local,
        mesh=mesh,
        in_specs=placed,
        out_specs=(P("seed", "feat"), P("feat", None), P("feat", None), P()),
        check_vma=False,
    )
```

profile of v0, /device:TPU:1, one launch (start us, length us, event | category | flops | bytes accessed | tf_op | source)
XLA Modules:
  0.0 485.6 jit_solution(5101217369946181815)
XLA Ops:
  7.2 0.0 copy-start
  7.2 3.2 copy.19
  10.4 0.8 compare_and_fusion
  11.2 0.8 copy.23
  12.0 32.9 %gather_fusion = bf16[8192,192]{1,0:T(8,128)(2,1)} fusion(bf16[4096,192]{1,0:T(8,128)(2,1)S(1)} %copy.19, s32[8192]{0:T(1024)S(1)} %broadcast_clamp_fusion), kind=kCustom, calls=%fused_computation | custom fusion | bytes 6324224 | tf_op jit(solution)/shard_map/jit(_take)/gather | solution.py:24
  45.0 5.5 %copy.20 = bf16[32,256,192]{1,2,0:T(8,128)(2,1)S(1)} copy(bf16[32,256,192]{2,1,0:T(8,128)(2,1)} %bitcast.23) | data formatting | bytes 6291456 | tf_op jit(solution)/shard_map/jit(_take)/gather | solution.py:24
  50.4 1.9 broadcast_select_fusion
  52.4 0.0 copy-start.5
  52.4 0.0 copy-start.6
  52.4 9.6 %all-to-all-start = ((bf16[32,256,192]{1,2,0:T(8,128)(2,1)}), bf16[32,256,192]{1,2,0:T(8,128)(2,1)S(1)}, u32[]{:S(2)}, u32[]{:S(2)}) async-start(bf16[32,256,192]{1,2,0:T(8,128)(2,1)} %broadcast_select_fusion), calls=%async_computation | async-start | bytes 6291456 | tf_op jit(solution)/shard_map/all_to_all | solution.py:26
  61.9 0.0 reduce-scatter.2.cloned.1.call-start
  62.0 0.8 broadcast_in_dim.23
  62.8 2.1 reshape.118
  64.9 1.9 copy.18
  66.9 2.1 reshape.119
  69.0 1.2 compare_select_fusion
  70.1 0.0 copy-done.5
  70.2 0.4 multiply_reduce_fusion
  70.6 0.0 copy-done.6
  70.6 0.5 and_reduce_fusion
  71.0 0.7 broadcast_select_fusion.1
  71.7 0.6 broadcast.77
  72.4 147.0 %scatter_custom_fusion = f32[8388608]{0:T(1024)} fusion(s32[25600]{0:T(1024)} %broadcast_select_fusion.1, f32[25600]{0:T(1024)} %broadcast.77, f32[]{:T(128)} %constant.12.clone.1), kind=kCustom, calls=%fused_computation.2 | custom fusion | flops 25600 | bytes 33554944
  219.4 17.1 %convert_element_type.22 = bf16[8388608]{0:T(1024)(128)(2,1)} convert(f32[8388608]{0:T(1024)} %scatter_custom_fusion) | non-fusion elementwise | flops 8388608 | bytes 50331648 | tf_op jit(solution)/shard_map/convert_element_type | solution.py:22
  236.5 25.3 %reshape.126 = bf16[1024,8192]{1,0:T(8,128)(2,1)} reshape(bf16[8388608]{0:T(1024)(128)(2,1)} %convert_element_type.22) | data formatting | bytes 33554432 | tf_op jit(solution)/shard_map/convert_element_type | solution.py:22
  261.8 0.0 all-to-all-done
  261.8 0.4 copy.22
  262.2 0.0 copy-start.4
  262.2 9.7 %convolution_multiply_fusion = f32[1024,192]{0,1:T(8,128)S(1)} fusion(bf16[1024,8192]{1,0:T(8,128)(2,1)} %reshape.126, bf16[8192,192]{0,1:T(8,128)(2,1)S(1)} %bitcast.25), kind=kOutput, calls=%fused_computation.8 | convolution fusion | flops 3221422080 | bytes 20709376 | tf_op jit(solution)/shard_map/dot_general | solution.py:27
  271.9 0.0 copy-done.4
  271.9 0.0 copy-start.3
  271.9 1.9 fusion.2
  273.9 0.0 copy-done
  273.9 0.0 copy-done.3
  273.9 2.7 convolution_add_fusion
  276.6 0.0 copy-start.2
  276.6 0.0 reduce-scatter.2.cloned.1.call-update
  276.6 0.0 all-gather.2.cloned.1.call-start
  276.7 0.8 dynamic_slice.3
  277.5 47.3 %reduce-scatter.2.cloned.1.call-done = f32[1024,256]{1,0:T(8,128)} async-done(((f32[1024,1024]{1,0:T(8,128)}), f32[1024,256]{1,0:T(8,128)}) %reduce-scatter.2.cloned.1.call-update) | async-done | bytes 1048592 | tf_op jit(solution)/shard_map/reduce_scatter | solution.py:33
  324.8 0.0 copy-done.2
  324.8 2.7 multiply_convert_fusion
  327.5 0.0 all-gather.2.cloned.1.call-update
  327.5 0.0 all-reduce.3.cloned.1.call-start
  327.6 33.4 %all-gather.2.cloned.1.call-done = bf16[1024,1024]{1,0:T(8,128)(2,1)} async-done(((bf16[1024,256]{1,0:T(8,128)(2,1)}), bf16[1024,1024]{1,0:T(8,128)(2,1)}) %all-gather.2.cloned.1.call-update) | async-done | bytes 2097168 | tf_op jit(solution)/shard_map/all_gather | solution.py:37
  361.0 0.0 copy-start.1
  361.0 4.0 fusion.3
  365.0 0.0 copy-done.1
  365.0 1.5 convolution_bitcast_fusion
  366.5 0.0 all-reduce.3.cloned.1.call-update
  366.5 0.4 convert_reduce_fusion
  366.9 64.4 %psum.23 = f32[1024]{0:T(1024)} all-reduce(f32[1024]{0:T(1024)S(1)} %convert_reduce_fusion), channel_id=1, replica_groups=mesh['feat'=4,'seed'=32] {'seed'}, use_global_device_ids=true, to_apply=%region_5.6 | all-reduce | flops 1024 | bytes 8192 | tf_op jit(solution)/shard_map/psum | solution.py:47
  431.3 43.6 %all-reduce.3.cloned.1.call-done = (f32[192,1024]{1,0:T(8,128)}, f32[192,1024]{1,0:T(8,128)}) async-done(((f32[192,1024]{1,0:T(8,128)}, f32[192,1024]{1,0:T(8,128)}), (f32[192,1024]{1,0:T(8,128)}, f32[192,1024]{1,0:T(8,128)})) %all-reduce.3.cloned.1.call-update) | async-done | bytes 1572880 | tf_op jit(solution)/shard_map/psum | solution.py:47
  474.9 2.1 copy.26
  477.0 2.1 copy.27
  (2 shorter events, 0.0 us)
Async XLA Ops:
  7.2 266.7 %copy-start = (bf16[192,1024]{1,0:T(8,128)(2,1)S(1)}, bf16[192,1024]{1,0:T(8,128)(2,1)}, u32[]{:S(2)}) copy-start(bf16[192,1024]{1,0:T(8,128)(2,1)} %param.9) | copy-start | bytes 1179652
  52.4 17.8 %copy-start.5 = (s32[2]{0:T(128)S(1)}, s32[2]{0:T(128)}, u32[]{:S(2)}) copy-start(s32[2]{0:T(128)} %constant.43) | copy-start | bytes 28
  52.4 18.2 %copy-start.6 = (s32[2]{0:T(128)S(1)}, s32[2]{0:T(128)}, u32[]{:S(2)}) copy-start(s32[2]{0:T(128)} %constant.46) | copy-start | bytes 28
  52.4 209.5 %all-to-all-start = ((bf16[32,256,192]{1,2,0:T(8,128)(2,1)}), bf16[32,256,192]{1,2,0:T(8,128)(2,1)S(1)}, u32[]{:S(2)}, u32[]{:S(2)}) async-start(bf16[32,256,192]{1,2,0:T(8,128)(2,1)} %broadcast_select_fusion), calls=%async_computation | async-start | bytes 6291456 | tf_op jit(solution)/shard_map/all_to_all | solution.py:26
  61.9 262.9 %reduce-scatter.2.cloned.1.call-start = ((), (), s32[]{:S(2)}) async-start(), calls=%async_computation.2 | async-start | bytes 5242880 | tf_op jit(solution)/shard_map/reduce_scatter | solution.py:33
  262.2 9.7 %copy-start.4 = (bf16[192,1024]{1,0:T(8,128)(2,1)S(1)}, bf16[192,1024]{1,0:T(8,128)(2,1)}, u32[]{:S(2)}) copy-start(bf16[192,1024]{1,0:T(8,128)(2,1)} %param.11) | copy-start | bytes 1179652
  271.9 2.0 copy-start.3
  276.6 48.2 %copy-start.2 = (bf16[1024,256]{1,0:T(8,128)(2,1)S(1)}, bf16[1024,256]{1,0:T(8,128)(2,1)}, u32[]{:S(2)}) copy-start(bf16[1024,256]{1,0:T(8,128)(2,1)} %param.15) | copy-start | bytes 1572868
  276.6 84.4 %all-gather.2.cloned.1.call-start = ((), (), s32[]{:S(2)}) async-start(), calls=%async_computation.3 | async-start | bytes 2621440 | tf_op jit(solution)/shard_map/all_gather | solution.py:37
  327.5 147.4 %all-reduce.3.cloned.1.call-start = ((), (), s32[]{:S(2)}) async-start(), calls=%async_computation.4 | async-start | bytes 3145728 | tf_op jit(solution)/shard_map/psum | solution.py:47
  361.0 4.1 copy-start.1
Sparse Core Ops, SparseCore 0:
  276.7 48.0 reduce-scatter.1
  327.6 33.2 all-gather.1
  366.6 108.2 all-reduce.2
where the time goes:
time: 487 us; the launch traced here: 486 us
  other arithmetic  173 us (36%)
  waiting for transfers between devices  124 us (25%)
  local copies, waits for them, and re-layouts  80.7 us (17%)
  blocking collectives  64.4 us (13%)
  matrix products  19.8 us (4%)
  between operations  13.9 us (3%)
  starting transfers between devices  9.69 us (2%)
    unnamed x4, other arithmetic  149 us
    psum x1, blocking collectives, local(): lax.psum((grad_self, grad_neigh, grad_bias), 'seed')  64.4 us
    reduce_scatter x1, waiting for transfers between devices, local(): lax.psum_scatter(partial_value, 'feat', scatter_dimension=1, tiled=True)  47.3 us
    psum x1, waiting for transfers between devices, local(): lax.psum((grad_self, grad_neigh, grad_bias), 'seed')  43.6 us
    gather x2, local copies, waits for them, and re-layouts, local(): picked = jnp.take(node_feats, send_list.reshape(-1), axis=0)  38.4 us
    all_gather x1, waiting for transfers between devices, local(): grad_pre = lax.all_gather(grad_share, 'feat', axis=1, tiled=True)  33.4 us
    convert_element_type x1, local copies, waits for them, and re-layouts, local(): counts = jnp.zeros((seed_rows, slot_rows), jnp.float32).at[owners, flat_s...  25.3 us
    convert_element_type x1, other arithmetic, local(): counts = jnp.zeros((seed_rows, slot_rows), jnp.float32).at[owners, flat_s...  17.1 us
  transfers between devices with their start and end apart: 4, of which 3 were waited for; matrix products, arithmetic and copies ran while one was open for 41% of the time, Pallas kernels for 0%

commit v1 on v0

v1 whole, which is shorter than its diff:
```python
import jax
import jax.numpy as jnp
from jax import lax
from jax.experimental import pallas as pl
from jax.experimental.pallas import tpu as pltpu
from jax.sharding import PartitionSpec as P

MESH = pl.DeviceIdType.MESH
BF, F32, I32 = jnp.bfloat16, jnp.float32, jnp.int32
NT = (((1,), (1,)), ((), ()))


def chip_order():
    steps = []
    for a, b in ((2, 2), (1, 2), (0, 2), (1, 1), (0, 1)):
        turn = []
        for p in ((a, b), (-b, a), (-a, -b), (b, -a)):
            p = (p[0] % 4, p[1] % 4)
            if p not in turn:
                turn.append(p)
        steps += [p + (core,) for core in (0, 1) for p in turn]
    return steps


STEPS = chip_order()


def pick(values, i):
    low = sum(v << (2 * k) for k, v in enumerate(values[:15]))
    high = sum(v << (2 * k) for k, v in enumerate(values[15:]))
    return (jnp.where(i < 15, low, high) >> (2 * (i % 15))) & 3


def offset(i):
    last = i >= 30
    dz = jnp.where(last, 0, pick([s[0] for s in STEPS], i))
    dx = jnp.where(last, 0, pick([s[1] for s in STEPS], i))
    dc = jnp.where(last, 1, pick([s[2] for s in STEPS], i))
    return dz, dx, dc


def kernel(
    node, seed, w_self, w_neigh, bias, send_list, nbr, cot,
    hid, g_self, g_neigh, g_bias,
    node_t, out_rows, in_rows, counts, acc, x_self, x_a1, x_a2, wr_self, wr_a1, wr_a2,
    pre, cot_t, hid_t, gp, grad, core_in, half, red2, part2, red3, part3, full,
    bias_parts, bias_red, bias_full,
    row_send, row_recv, y_send, y_recv, d_send, d_recv,
):
    y = lax.axis_index("feat")
    me = lax.axis_index("seed")
    z, x, c = me // 8, (me // 2) % 4, me % 2

    def seed_id(z2, x2, c2):
        return (z2 * 4 + x2) * 2 + c2

    def at(feat, seed_index):
        return {"feat": feat, "seed": seed_index}

    def target(i):
        dz, dx, dc = offset(i)
        oz = jnp.where(c == 1, -dx, dz)
        ox = jnp.where(c == 1, dz, dx)
        return seed_id((z + oz + 4) % 4, (x + ox + 4) % 4, (c + dc) % 2)

    def source(i):
        dz, dx, dc = offset(i)
        c2 = (c + dc) % 2
        oz = jnp.where(c2 == 1, -dx, dz)
        ox = jnp.where(c2 == 1, dz, dx)
        return seed_id((z - oz + 4) % 4, (x - ox + 4) % 4, c2)

    barrier = pltpu.get_barrier_semaphore()

    def greet(t, _):
        pl.semaphore_signal(
            barrier, inc=1, device_id=at(y, (me + t) % 32), device_id_type=MESH
        )
        return 0

    lax.fori_loop(1, 32, greet, 0)
    for k in (1, 2, 3):
        pl.semaphore_signal(
            barrier, inc=1, device_id=at((y + k) % 4, me), device_id_type=MESH
        )

    for j in range(16):
        block = node[j * 256 : (j + 1) * 256, :].T
        for q in range(3):
            start = q * 1024 + j * 64
            node_t[start : start + 64, :] = block[q * 64 : (q + 1) * 64, :]

    pl.semaphore_wait(barrier, 34)

    def y_copy(kind, src, dst, peer):
        return pltpu.make_async_remote_copy(
            src_ref=src,
            dst_ref=dst,
            send_sem=y_send.at[kind, peer],
            recv_sem=y_recv.at[kind, y],
            device_id=at(peer, me),
            device_id_type=MESH,
        )

    def y_arrival(kind, src, dst, peer):
        return pltpu.make_async_remote_copy(
            src_ref=src,
            dst_ref=dst,
            send_sem=y_send.at[kind, peer],
            recv_sem=y_recv.at[kind, peer],
            device_id=at(peer, me),
            device_id_type=MESH,
        )

    def cols(peer):
        return pl.ds(pl.multiple_of(peer * 256, 256), 256)

    peers = [(y + k) % 4 for k in (1, 3, 2)]
    for peer in peers:
        y_copy(0, w_self.at[:, cols(peer)], wr_self.at[y], peer).start()
        y_copy(1, w_neigh.at[pl.ds(0, 128), cols(peer)], wr_a1.at[y], peer).start()
        y_copy(2, w_neigh.at[pl.ds(128, 64), cols(peer)], wr_a2.at[y], peer).start()
    for peer in peers:
        y_copy(3, seed, x_self.at[y], peer).start()
    wr_self[y] = w_self[:, cols(y)]
    wr_a1[y] = w_neigh[0:128, cols(y)]
    wr_a2[y] = w_neigh[128:192, cols(y)]
    x_self[y] = seed[...]

    def row_copy(part, to, sender):
        rows = pl.ds(0, 128) if part == 0 else pl.ds(128, 64)
        return pltpu.make_async_remote_copy(
            src_ref=out_rows.at[to, rows],
            dst_ref=in_rows.at[sender, rows],
            send_sem=row_send.at[part, to],
            recv_sem=row_recv.at[part, sender],
            device_id=at(y, to),
            device_id_type=MESH,
        )

    ids = lax.broadcasted_iota(I32, (256, 256), 0)
    in_group = lax.broadcasted_iota(I32, (1, 256), 1) // 32

    def one_hot(row):
        return jnp.where(ids == row, 1.0, 0.0).astype(BF)

    def gather_step(i, _):
        to = jnp.where(i == 31, me, target(i))
        index = send_list[pl.ds(to, 1), :]
        block, chosen = index // 256, one_hot(index % 256)
        for q in range(3):
            every = jnp.dot(
                node_t[q * 1024 : (q + 1) * 1024, :], chosen, preferred_element_type=F32
            )
            rows = jnp.zeros((64, 256), F32)
            for j in range(16):
                rows = jnp.where(block == j, every[j * 64 : (j + 1) * 64], rows)
            out_rows[to, q * 64 : (q + 1) * 64, :] = rows.astype(BF)

        @pl.when(i < 31)
        def _():
            row_copy(0, to, me).start()

        for e in range(2):
            group = 2 * i + e
            found = []
            for h in range(2):
                slot = nbr[pl.ds(2 * group + h, 1), :]
                key = jnp.where(slot < 0, -1, (slot // 256) * 8 + in_group)
                hits = lax.dot_general(
                    one_hot(key), one_hot(slot % 256), NT, preferred_element_type=F32
                )
                found.append(hits.reshape(32, 8, 256))
            counts[:, pl.ds(pl.multiple_of(group * 16, 16), 16), :] = jnp.concatenate(
                found, axis=1
            ).astype(BF)
        return 0

    lax.fori_loop(0, 32, gather_step, 0)

    def second_step(i, _):
        row_copy(1, target(i), me).start()
        return 0

    lax.fori_loop(0, 31, second_step, 0)

    def add_up(part):
        lo, n = (0, 128) if part == 0 else (128, 64)

        def term(rows, sender):
            return lax.dot_general(
                rows, counts[sender], NT, preferred_element_type=F32
            )

        def arrived(i):
            sender = source(i)
            row_copy(part, sender, sender).wait_recv()
            return term(in_rows[sender, lo : lo + n, :], sender)

        first = term(out_rows[me, lo : lo + n, :], me)
        for i in range(3):
            first = first + arrived(i)
        acc[lo : lo + n, :] = first

        def four(g, _):
            more = arrived(4 * g + 3)
            for i in range(1, 4):
                more = more + arrived(4 * g + 3 + i)
            acc[lo : lo + n, :] += more
            return 0

        lax.fori_loop(0, 7, four, 0)
        return (acc[lo : lo + n, :] * (1.0 / 25.0)).astype(BF)

    x_a1[y] = add_up(0)
    for peer in peers:
        y_copy(4, x_a1.at[y], x_a1.at[y], peer).start()

    for peer in peers:
        y_arrival(0, w_self.at[:, cols(peer)], wr_self.at[peer], peer).wait_recv()
        y_arrival(3, seed, x_self.at[peer], peer).wait_recv()
    own_bias = jnp.broadcast_to(bias[:, cols(y)], (128, 256)).T
    own_bias = jnp.concatenate([own_bias] * 8, axis=1)
    pre[...] = own_bias + jnp.dot(
        wr_self[...].reshape(768, 256).T,
        x_self[...].reshape(768, 1024),
        preferred_element_type=F32,
    )
    cot_t[...] = cot[...].T.astype(F32)

    x_a2[y] = add_up(1)
    for peer in peers:
        y_copy(5, x_a2.at[y], x_a2.at[y], peer).start()

    for peer in peers:
        y_arrival(1, w_neigh.at[pl.ds(0, 128), cols(peer)], wr_a1.at[peer], peer).wait_recv()
        y_arrival(2, w_neigh.at[pl.ds(128, 64), cols(peer)], wr_a2.at[peer], peer).wait_recv()
        y_arrival(4, x_a1.at[peer], x_a1.at[peer], peer).wait_recv()
    pre[...] += jnp.dot(
        wr_a1[...].reshape(512, 256).T,
        x_a1[...].reshape(512, 1024),
        preferred_element_type=F32,
    )
    for peer in peers:
        y_arrival(5, x_a2.at[peer], x_a2.at[peer], peer).wait_recv()
    pre[...] += jnp.dot(
        wr_a2[...].reshape(256, 256).T,
        x_a2[...].reshape(256, 1024),
        preferred_element_type=F32,
    )

    def activate(b, _):
        rows = pl.ds(pl.multiple_of(b * 32, 32), 32)
        v = pre[rows, :]
        s = 1.0 / (1.0 + jnp.exp(-v))
        hid_t[rows, :] = (v * s).astype(BF)
        gp[rows, :] = (cot_t[rows, :] * (s * (1.0 + v * (1.0 - s)))).astype(BF)
        return 0

    lax.fori_loop(0, 8, activate, 0)

    def weigh(b, _):
        for source_rows, lo, n in ((x_self, 0, 192), (x_a1, 192, 128), (x_a2, 320, 64)):
            value = lax.dot_general(
                source_rows[b], gp[...], NT, preferred_element_type=F32
            )
            rows = pl.ds(pl.multiple_of(b * 384 + lo, 64), n)
            grad[0, rows, :] = value[:, :128]
            grad[1, rows, :] = value[:, 128:]
        return 0

    lax.fori_loop(0, 4, weigh, 0)
    ones = jnp.ones((16, 1024), BF)
    bias_parts[0] = lax.dot_general(ones, gp[...], NT, preferred_element_type=F32)[:8]

    def d_copy(kind, src, dst, to_sem, from_sem, device):
        return pltpu.make_async_remote_copy(
            src_ref=src,
            dst_ref=dst,
            send_sem=d_send.at[kind, to_sem],
            recv_sem=d_recv.at[kind, from_sem],
            device_id=device,
            device_id_type=MESH,
        )

    other = at(y, seed_id(z, x, 1 - c))
    ahead = (1, 3, 2)

    def along_x(x2):
        return at(y, seed_id(z, x2, c))

    def along_z(z2):
        return at(y, seed_id(z2, x, c))

    core_copy = d_copy(0, grad.at[1 - c], core_in, 0, 0, other)
    core_bias = d_copy(1, bias_parts.at[0], bias_red.at[0], 0, 0, other)
    core_copy.start()
    core_bias.start()
    hid[...] = hid_t[...].T
    core_copy.wait_recv()
    core_bias.wait_recv()
    half[...] = (grad[c] + core_in[...]).reshape(4, 384, 128)
    bias_parts[1] = bias_parts[0] + bias_red[0]

    def piece(i, n):
        return pl.ds(pl.multiple_of(i * n, n), n)

    orders = ((x, along_x, z, along_z), (z, along_z, x, along_x))
    sent = [core_copy, core_bias]
    for k in ahead:
        for o, (mine, along, _, _) in enumerate(orders):
            to = (mine + k) % 4
            copy = d_copy(
                2 + o, half.at[pl.ds(2 * o, 2), piece(to, 96)], red2.at[o, mine], to, mine, along(to)
            )
            copy.start()
            sent.append(copy)
        to = (x + k) % 4
        copy = d_copy(4, bias_parts.at[1], bias_red.at[1 + x], to, x, along_x(to))
        copy.start()
        sent.append(copy)
    for o, (mine, along, _, _) in enumerate(orders):
        total = half[2 * o : 2 * o + 2, piece(mine, 96), :]
        for k in ahead:
            fr = (mine + k) % 4
            d_copy(
                2 + o, half.at[pl.ds(2 * o, 2), piece(fr, 96)], red2.at[o, fr], fr, fr, along(fr)
            ).wait_recv()
            total = total + red2[o, fr]
        part2[o] = total
    total = bias_parts[1]
    for k in ahead:
        fr = (x + k) % 4
        d_copy(4, bias_parts.at[1], bias_red.at[1 + fr], fr, fr, along_x(fr)).wait_recv()
        total = total + bias_red[1 + fr]
    bias_parts[2] = total

    for k in ahead:
        for o, (_, _, mine, along) in enumerate(orders):
            to = (mine + k) % 4
            copy = d_copy(
                5 + o, part2.at[o, :, piece(to, 24)], red3.at[o, mine], to, mine, along(to)
            )
            copy.start()
            sent.append(copy)
        to = (z + k) % 4
        copy = d_copy(7, bias_parts.at[2], bias_red.at[5 + z], to, z, along_z(to))
        copy.start()
        sent.append(copy)
    for o, (_, _, mine, along) in enumerate(orders):
        total = part2[o, :, piece(mine, 24), :]
        for k in ahead:
            fr = (mine + k) % 4
            d_copy(
                5 + o, part2.at[o, :, piece(fr, 24)], red3.at[o, fr], fr, fr, along(fr)
            ).wait_recv()
            total = total + red3[o, fr]
        part3[2 * o : 2 * o + 2] = total
    total = bias_parts[2]
    for k in ahead:
        fr = (z + k) % 4
        d_copy(7, bias_parts.at[2], bias_red.at[5 + fr], fr, fr, along_z(fr)).wait_recv()
        total = total + bias_red[5 + fr]
    bias_full[y] = total

    def first_axis(feat):
        return jnp.where(feat < 2, x, z)

    def second_axis(feat):
        return jnp.where(feat < 2, z, x)

    for k in ahead:
        to = (y + k) % 4
        copy = d_copy(
            8, part3.at[to], full.at[c, first_axis(to), second_axis(to), y], to, y, at(to, me)
        )
        copy.start()
        sent.append(copy)
        copy = d_copy(9, bias_full.at[y], bias_full.at[y], to, y, at(to, me))
        copy.start()
        sent.append(copy)
    i, j = first_axis(y), second_axis(y)
    full[c, i, j, y] = part3[y]
    for k in ahead:
        fr = (y + k) % 4
        d_copy(8, part3.at[fr], full.at[c, i, j, fr], fr, fr, at(fr, me)).wait_recv()
        d_copy(9, bias_full.at[fr], bias_full.at[fr], fr, fr, at(fr, me)).wait_recv()

    def along_first(i2):
        return at(y, jnp.where(y < 2, seed_id(z, i2, c), seed_id(i2, x, c)))

    def along_second(j2):
        return at(y, jnp.where(y < 2, seed_id(j2, x, c), seed_id(z, j2, c)))

    a, b = pl.ds(0, 2), pl.ds(2, 2)
    for k in ahead:
        to = (j + k) % 4
        copy = d_copy(10, full.at[c, i, j, a], full.at[c, i, j, a], to, j, along_second(to))
        copy.start()
        sent.append(copy)
        to = (i + k) % 4
        copy = d_copy(11, full.at[c, i, j, b], full.at[c, i, j, b], to, i, along_first(to))
        copy.start()
        sent.append(copy)
    for k in ahead:
        fr = (j + k) % 4
        d_copy(10, full.at[c, i, j, a], full.at[c, i, fr, a], fr, fr, along_second(fr)).wait_recv()
        fr = (i + k) % 4
        d_copy(11, full.at[c, i, j, b], full.at[c, fr, j, b], fr, fr, along_first(fr)).wait_recv()
    for k in ahead:
        to = (i + k) % 4
        copy = d_copy(12, full.at[c, i, :, a], full.at[c, i, :, a], to, i, along_first(to))
        copy.start()
        sent.append(copy)
        to = (j + k) % 4
        copy = d_copy(13, full.at[c, :, j, b], full.at[c, :, j, b], to, j, along_second(to))
        copy.start()
        sent.append(copy)
    for k in ahead:
        fr = (i + k) % 4
        d_copy(12, full.at[c, i, :, a], full.at[c, fr, :, a], fr, fr, along_first(fr)).wait_recv()
        fr = (j + k) % 4
        d_copy(13, full.at[c, :, j, b], full.at[c, :, fr, b], fr, fr, along_second(fr)).wait_recv()
    copy = d_copy(14, full.at[c], full.at[c], 0, 0, other)
    copy.start()
    sent.append(copy)
    d_copy(14, full.at[c], full.at[1 - c], 0, 0, other).wait_recv()

    for p in range(16):
        ref, row = (g_self, 24 * p) if p < 8 else (g_neigh, 24 * (p - 8))
        for q in range(8):
            ref[row : row + 24, q * 128 : (q + 1) * 128] = full[q % 2, p // 4, p % 4, q // 2]
    for q in range(4):
        g_bias[:, q * 256 : (q + 1) * 256] = bias_full[q, 0:1, :]

    for copy in sent:
        copy.wait_send()
    for peer in peers:
        y_copy(0, w_self.at[:, cols(peer)], wr_self.at[y], peer).wait_send()
        y_copy(1, w_neigh.at[pl.ds(0, 128), cols(peer)], wr_a1.at[y], peer).wait_send()
        y_copy(2, w_neigh.at[pl.ds(128, 64), cols(peer)], wr_a2.at[y], peer).wait_send()
        y_copy(3, seed, x_self.at[y], peer).wait_send()
        y_copy(4, x_a1.at[y], x_a1.at[y], peer).wait_send()
        y_copy(5, x_a2.at[y], x_a2.at[y], peer).wait_send()

    def left(i, _):
        row_copy(0, target(i), me).wait_send()
        row_copy(1, target(i), me).wait_send()
        return 0

    lax.fori_loop(0, 31, left, 0)


def local(node_feats, seed_feats, w_self, w_neigh, bias, send_list, nbr_slot, cotangent):
    nbr = jnp.pad(nbr_slot, ((0, 0), (0, 7)), constant_values=-1).reshape(128, 256)
    vmem = pl.BlockSpec(memory_space=pltpu.VMEM)
    V, DMA = pltpu.VMEM, pltpu.SemaphoreType.DMA
    hidden, grad_self, grad_neigh, grad_bias = pl.pallas_call(
        kernel,
        out_shape=(
            jax.ShapeDtypeStruct((1024, 256), BF),
            jax.ShapeDtypeStruct((192, 1024), F32),
            jax.ShapeDtypeStruct((192, 1024), F32),
            jax.ShapeDtypeStruct((1, 1024), F32),
        ),
        in_specs=[vmem] * 8,
        out_specs=(vmem,) * 4,
        scratch_shapes=[
            V((3072, 256), BF),
            V((32, 192, 256), BF),
            V((32, 192, 256), BF),
            V((32, 1024, 256), BF),
            V((192, 1024), F32),
            V((4, 192, 1024), BF),
            V((4, 128, 1024), BF),
            V((4, 64, 1024), BF),
            V((4, 192, 256), BF),
            V((4, 128, 256), BF),
            V((4, 64, 256), BF),
            V((256, 1024), F32),
            V((256, 1024), F32),
            V((256, 1024), BF),
            V((256, 1024), BF),
            V((2, 1536, 128), F32),
            V((1536, 128), F32),
            V((4, 384, 128), F32),
            V((2, 4, 2, 96, 128), F32),
            V((2, 2, 96, 128), F32),
            V((2, 4, 2, 24, 128), F32),
            V((4, 24, 128), F32),
            V((2, 4, 4, 4, 24, 128), F32),
            V((3, 8, 256), F32),
            V((9, 8, 256), F32),
            V((4, 8, 256), F32),
            DMA((2, 32)),
            DMA((2, 32)),
            DMA((6, 4)),
            DMA((6, 4)),
            DMA((15, 4)),
            DMA((15, 4)),
        ],
        compiler_params=pltpu.CompilerParams(
            collective_id=0, has_side_effects=True, vmem_limit_bytes=60 << 20
        ),
        name="sage_layer",
    )(
        node_feats,
        seed_feats,
        w_self,
        w_neigh,
        bias.reshape(1, 1024),
        send_list.reshape(32, 256),
        nbr,
        cotangent,
    )
    return hidden, grad_self, grad_neigh, grad_bias.reshape(1024)


def solution(mesh):
    placed = (
        P("seed", "feat"),
        P("feat", "seed"),
        P("feat", None),
        P("feat", None),
        P(),
        P("seed", None, None),
        P("seed", None),
        P("seed", "feat"),
    )
    return jax.shard_map(
        local,
        mesh=mesh,
        in_specs=placed,
        out_specs=(P("seed", "feat"), P("feat", None), P("feat", None), P()),
        check_vma=False,
    )
```

time: 487 us -> 126 us (0.26)
  other arithmetic: 173 us -> 0 us
  waiting for transfers between devices: 124 us -> 0 us
  Pallas kernels: 0 us -> 115 us
  local copies, waits for them, and re-layouts: 80.7 us -> 10.1 us
  blocking collectives: 64.4 us -> 0 us
  matrix products: 19.8 us -> 0 us
  between operations: 13.9 us -> 0.68 us
  starting transfers between devices: 9.69 us -> 0 us
    unnamed x4 -> x0, other arithmetic: 149 us -> none
    pallas_call x0 -> x1, Pallas kernels: none -> 115 us  [local(): pl.pallas_call(kernel, out_shape=(jax.ShapeDtypeStruct((1024, 256), BF),...]
    psum x1 -> x0, blocking collectives: 64.4 us -> none  [local(): lax.psum((grad_self, grad_neigh, grad_bias), 'seed')]
    reduce_scatter x1 -> x0, waiting for transfers between devices: 47.3 us -> none  [local(): lax.psum_scatter(partial_value, 'feat', scatter_dimension=1, tiled=True)]
    psum x1 -> x0, waiting for transfers between devices: 43.6 us -> none  [local(): lax.psum((grad_self, grad_neigh, grad_bias), 'seed')]
    gather x2 -> x0, local copies, waits for them, and re-layouts: 38.4 us -> none  [local(): picked = jnp.take(node_feats, send_list.reshape(-1), axis=0)]
    all_gather x1 -> x0, waiting for transfers between devices: 33.4 us -> none  [local(): grad_pre = lax.all_gather(grad_share, 'feat', axis=1, tiled=True)]
    convert_element_type x1 -> x0, local copies, waits for them, and re-layouts: 25.3 us -> none  [local(): counts = jnp.zeros((seed_rows, slot_rows), jnp.float32).at[owners, flat_s...]
  transfers between devices with their start and end apart: 4 -> 0, of which waited for: 3 -> 0; matrix products, arithmetic and copies ran while one was open for 41% -> 0% of each run, Pallas kernels for 0% -> 0%
where the time goes in v1:
time: 126 us; the launch traced here: 125 us
  Pallas kernels  115 us (91%)
  local copies, waits for them, and re-layouts  10.1 us (8%)
    pallas_call x1, Pallas kernels, local(): pl.pallas_call(kernel, out_shape=(jax.ShapeDtypeStruct((1024, 256), BF),...  115 us
    unnamed x12, local copies, waits for them, and re-layouts  9.17 us

profile of v1, /device:TPU:1, one launch (start us, length us, event | category | flops | bytes accessed | tf_op | source)
XLA Modules:
  0.0 125.3 jit_solution(374674498462354424)
XLA Ops:
  0.6 0.0 copy-start
  0.6 1.2 copy.16
  1.9 0.8 reshape.22.nbr
  2.8 0.0 copy-done
  2.8 2.4 %copy.15.node = bf16[4096,192]{1,0:T(8,128)(2,1)} copy(bf16[4096,192]{0,1:T(8,128)(2,1)S(1)} %copy-done) | data formatting | bytes 3145728 | tf_op args[0]
  5.2 114.6 %sage_layer.1 = (bf16[1024,256]{1,0:T(8,128)(2,1)}, f32[192,1024]{1,0:T(8,128)}, f32[192,1024]{1,0:T(8,128)}, f32[1,1024]{1,0:T(1,128)}) custom-call(bf16[4096,192]{1,0:T(8,128)(2,1)} %copy.15.node, bf16[192,1024]{1,0:T(8,128)(2,1)} %seed.1, bf16[192,1024]{1,0:T(8,128)(2,1)} %w_self.1, bf16[192,1024]{1,0:T(8,128)(2,1)} %w_neigh.1, f32[1,1024]{1,0:T(1,128)} %bitcast.4, ...), custom_call_target="tpu_custom_call" | custom-call | tf_op jit(solution)/shard_map/sage_layer/pallas_call | solution.py:458
  119.8 0.0 copy-start.1
  119.8 0.0 copy-start.2
  119.8 1.9 %copy.21 = bf16[1024,256]{1,0:T(8,128)(2,1)} copy(bf16[1024,256]{1,0:T(8,128)(2,1)} %get-tuple-element.16) | data formatting | bytes 1048576
  121.8 2.1 %copy.22 = f32[192,1024]{1,0:T(8,128)} copy(f32[192,1024]{1,0:T(8,128)} %get-tuple-element.17) | data formatting | bytes 1572864
  123.9 0.0 copy-done.1
  123.9 0.9 copy.23
  124.7 0.0 copy-done.2
  124.7 0.6 copy.24
  (1 shorter events, 0.0 us)
Async XLA Ops:
  0.6 2.1 %copy-start = (bf16[4096,192]{0,1:T(8,128)(2,1)S(1)}, bf16[4096,192]{0,1:T(8,128)(2,1)}, u32[]{:S(2)}) copy-start(bf16[4096,192]{0,1:T(8,128)(2,1)} %param.8) | copy-start | bytes 4718596
  119.8 4.0 %copy-start.1 = (f32[192,1024]{1,0:T(8,128)S(1)}, f32[192,1024]{1,0:T(8,128)}, u32[]{:S(2)}) copy-start(f32[192,1024]{1,0:T(8,128)} %get-tuple-element.18) | copy-start | bytes 2359300
  119.8 4.9 %copy-start.2 = (f32[1,1024]{1,0:T(1,128)S(1)}, f32[1,1024]{1,0:T(1,128)}, u32[]{:S(2)}) copy-start(f32[1,1024]{1,0:T(1,128)} %get-tuple-element.11) | copy-start | bytes 12292

commit v2 on v1

v2 whole, which is shorter than its diff:
```python
import jax
import jax.numpy as jnp
from jax import lax
from jax.experimental import pallas as pl
from jax.experimental.pallas import tpu as pltpu
from jax.sharding import PartitionSpec as P

MESH = pl.DeviceIdType.MESH
BF, F32, I32 = jnp.bfloat16, jnp.float32, jnp.int32
NT = (((1,), (1,)), ((), ()))


def chip_order():
    steps = []
    for a, b in ((2, 2), (1, 2), (0, 2), (1, 1), (0, 1)):
        for p in ((a, b), (-b, a), (-a, -b), (b, -a)):
            p = (p[0] % 4, p[1] % 4)
            if p not in steps:
                steps.append(p)
    return steps


STEPS = chip_order()


def offset(i):
    at = 2 * (i % 16)
    dz = (sum(s[0] << (2 * k) for k, s in enumerate(STEPS)) >> at) & 3
    dx = (sum(s[1] << (2 * k) for k, s in enumerate(STEPS)) >> at) & 3
    return dz, dx, jnp.where(i >= 15, 1, 0)


def kernel(
    node, seed, w_self, w_neigh, bias, send_list, nbr, cot,
    hid, g_self, g_neigh, g_bias,
    node_t, slots, groups, out_rows, in_rows, counts, acc, x_self, x_a, wr_self, wr_a,
    pre, cot_t, hid_t, gp, grad, core_in, half, red2, part2, red3, part3, done, full,
    bias_parts, bias_red, bias_full,
    row_send, row_recv, y_send, y_recv, d_send, d_recv,
    chip_send, chip_recv, core_send, core_recv,
):
    y = lax.axis_index("feat")
    me = lax.axis_index("seed")
    z, x, c = me // 8, (me // 2) % 4, me % 2

    def seed_id(z2, x2, c2):
        return (z2 * 4 + x2) * 2 + c2

    def at(feat, seed_index):
        return {"feat": feat, "seed": seed_index}

    def target(i):
        dz, dx, dc = offset(i)
        oz = jnp.where(c == 1, -dx, dz)
        ox = jnp.where(c == 1, dz, dx)
        return seed_id((z + oz + 4) % 4, (x + ox + 4) % 4, (c + dc) % 2)

    def source(i):
        dz, dx, dc = offset(i)
        c2 = (c + dc) % 2
        oz = jnp.where(c2 == 1, -dx, dz)
        ox = jnp.where(c2 == 1, dz, dx)
        return seed_id((z - oz + 4) % 4, (x - ox + 4) % 4, c2)

    barrier = pltpu.get_barrier_semaphore()

    def greet(t, _):
        pl.semaphore_signal(
            barrier, inc=1, device_id=at(y, (me + t) % 32), device_id_type=MESH
        )
        return 0

    lax.fori_loop(1, 32, greet, 0)
    for k in (1, 2, 3):
        pl.semaphore_signal(
            barrier, inc=1, device_id=at((y + k) % 4, me), device_id_type=MESH
        )

    for j in range(16):
        for q in range(3):
            start = q * 1024 + j * 64
            node_t[start : start + 64, :] = node[
                q * 64 : (q + 1) * 64, j * 256 : (j + 1) * 256
            ]

    slots[...] = jnp.concatenate(
        [nbr[...], jnp.full((103, 1024), -1, I32)], axis=0
    ).T
    lane_group = lax.broadcasted_iota(I32, (128, 128), 1) // 32
    for part in range(2):
        line = slots[pl.ds(4 * part, 128, stride=8), :]
        for k in (1, 2, 3):
            moved = pltpu.roll(slots[pl.ds(4 * part + k, 128, stride=8), :], 32 * k, 1)
            line = jnp.where(lane_group == k, moved, line)
        groups[:, part * 128 : (part + 1) * 128] = line

    pl.semaphore_wait(barrier, 34)

    def y_copy(kind, src, dst, peer):
        return pltpu.make_async_remote_copy(
            src_ref=src,
            dst_ref=dst,
            send_sem=y_send.at[kind, peer],
            recv_sem=y_recv.at[kind, y],
            device_id=at(peer, me),
            device_id_type=MESH,
        )

    def y_arrival(kind, src, dst, peer):
        return pltpu.make_async_remote_copy(
            src_ref=src,
            dst_ref=dst,
            send_sem=y_send.at[kind, peer],
            recv_sem=y_recv.at[kind, peer],
            device_id=at(peer, me),
            device_id_type=MESH,
        )

    def cols(peer):
        return pl.ds(pl.multiple_of(peer * 256, 256), 256)

    def half_cols(peer, core):
        return pl.ds(pl.multiple_of(peer * 256 + core * 128, 128), 128)

    peers = [(y + k) % 4 for k in (1, 3, 2)]
    up, down, across = peers
    side = half_cols(0, c)
    other = at(y, seed_id(z, x, 1 - c))

    def seed_copy(peer):
        return y_copy(2, seed, x_self.at[y], peer)

    def w_copies(peer):
        own = half_cols(peer, c)
        return (
            y_copy(0, w_self.at[:, own], wr_self.at[y, :, side], peer),
            y_copy(1, w_neigh.at[:, :, own], wr_a.at[:, y, :, side], peer),
        )

    def seed_onward(way):
        fr, to, rows = (down, up, pl.ds(0, 96)) if way == 0 else (up, down, pl.ds(96, 96))
        return pltpu.make_async_remote_copy(
            src_ref=x_self.at[fr, rows],
            dst_ref=x_self.at[fr, rows],
            send_sem=y_send.at[6, way],
            recv_sem=y_recv.at[6, way],
            device_id=at(to, me),
            device_id_type=MESH,
        )

    def seed_onward_arrival(way):
        rows = pl.ds(0, 96) if way == 0 else pl.ds(96, 96)
        return pltpu.make_async_remote_copy(
            src_ref=x_self.at[across, rows],
            dst_ref=x_self.at[across, rows],
            send_sem=y_send.at[6, way],
            recv_sem=y_recv.at[6, way],
            device_id=at(up, me),
            device_id_type=MESH,
        )

    def w_to_core(kind, peer, core):
        part = half_cols(0, core)
        ref = wr_self.at[peer, :, part] if kind == 7 else wr_a.at[:, peer, :, part]
        return pltpu.make_async_remote_copy(
            src_ref=ref,
            dst_ref=ref,
            send_sem=y_send.at[kind, peer],
            recv_sem=y_recv.at[kind, peer],
            device_id=other,
            device_id_type=MESH,
        )

    for peer in (up, down):
        seed_copy(peer).start()
    for peer in peers:
        for copy in w_copies(peer):
            copy.start()
    wr_self[y] = w_self[:, cols(y)]
    for part in range(3):
        wr_a[part, y] = w_neigh[part, :, cols(y)]
    x_self[y] = seed[...]

    def row_copy(part, to, sender):
        rows = pl.ds(0, 192) if part == 3 else pl.ds(64 * part, 64)
        return pltpu.make_async_remote_copy(
            src_ref=out_rows.at[to, rows],
            dst_ref=in_rows.at[sender, rows],
            send_sem=row_send.at[part, to],
            recv_sem=row_recv.at[part, sender],
            device_id=at(y, to),
            device_id_type=MESH,
        )

    ids = lax.broadcasted_iota(I32, (256, 256), 0)
    in_group = lax.broadcasted_iota(I32, (1, 256), 1) // 32

    def one_hot(row):
        return jnp.where(ids == row, 1.0, 0.0).astype(BF)

    def gather(part, to):
        index = send_list[pl.ds(to, 1), :]
        block, chosen = index // 256, one_hot(index % 256)
        every = jnp.dot(
            node_t[part * 1024 : (part + 1) * 1024, :], chosen, preferred_element_type=F32
        )
        rows = jnp.zeros((64, 256), F32)
        for j in range(16):
            rows = jnp.where(block == j, every[j * 64 : (j + 1) * 64], rows)
        out_rows[to, part * 64 : (part + 1) * 64, :] = rows.astype(BF)

    def count(i):
        for e in range(4):
            group = 4 * i + e
            found = []
            for h in range(2):
                slot = groups[pl.ds(2 * group + h, 1), :]
                key = jnp.where(slot < 0, -1, (slot // 256) * 8 + in_group)
                hits = lax.dot_general(
                    one_hot(key), one_hot(slot % 256), NT, preferred_element_type=F32
                )
                found.append(hits.reshape(32, 8, 256))
            counts[:, pl.ds(pl.multiple_of(group * 16, 16), 16), :] = jnp.concatenate(
                found, axis=1
            ).astype(BF)

    def span(part):
        return slice(0, 192) if part == 3 else slice(64 * part, 64 * part + 64)

    def own_term(part):
        return lax.dot_general(
            out_rows[me, span(part), :], counts[me], NT, preferred_element_type=F32
        )

    def terms(part, steps):
        senders = [source(i) for i in steps]
        for sender in senders:
            row_copy(part, sender, sender).wait_recv()
        total = None
        for sender in senders:
            more = lax.dot_general(
                in_rows[sender, span(part), :], counts[sender], NT, preferred_element_type=F32
            )
            total = more if total is None else total + more
        return total

    def early_step(g, _):
        to = [target(2 * g + k) for k in range(2)]
        for k in range(2):
            for part in range(3):
                gather(part, to[k])
            count(2 * g + k)
        for k in range(2):
            row_copy(3, to[k], me).start()
        return 0

    def late_target(i):
        return jnp.where(i == 31, me, target(i))

    def late_send(part, i, to):
        @pl.when(i < 31)
        def _():
            row_copy(part, to, me).start()

    def late_first(g, _):
        steps = [16 + 4 * g + k for k in range(4)]
        to = [late_target(i) for i in steps]
        early = terms(3, [4 * g + k for k in range(4)])
        for k in range(4):
            gather(0, to[k])
        acc[...] += early
        for k in range(4):
            late_send(0, steps[k], to[k])
        return 0

    def late_rest(g, _):
        steps = [16 + 4 * g + k for k in range(4)]
        to = [late_target(i) for i in steps]
        for k in range(4):
            gather(1, to[k])
            gather(2, to[k])
        for k in range(4):
            late_send(1, steps[k], to[k])
        return 0

    def late_last(i, _):
        row_copy(2, target(i), me).start()
        return 0

    acc[...] = jnp.zeros((192, 1024), F32)
    lax.fori_loop(0, 8, early_step, 0)
    lax.fori_loop(0, 4, late_first, 0)
    for peer in (up, down):
        y_arrival(2, seed, x_self.at[peer], peer).wait_recv()
    for way in range(2):
        seed_onward(way).start()
    for peer in peers:
        own = half_cols(peer, c)
        y_arrival(0, w_self.at[:, own], wr_self.at[peer, :, side], peer).wait_recv()
        y_arrival(1, w_neigh.at[:, :, own], wr_a.at[:, peer, :, side], peer).wait_recv()
        w_to_core(7, peer, c).start()
        w_to_core(8, peer, c).start()
    lax.fori_loop(0, 4, late_rest, 0)
    lax.fori_loop(16, 31, late_last, 0)

    def add_up(part):
        rows = span(part)
        acc[rows, :] += own_term(part)

        def five(g, _):
            acc[rows, :] += terms(part, [16 + 5 * g + k for k in range(5)])
            return 0

        lax.fori_loop(0, 3, five, 0)
        x_a[part, y] = (acc[rows, :] * (1.0 / 25.0)).astype(BF)
        for peer in peers:
            y_copy(3 + part, x_a.at[part, y], x_a.at[part, y], peer).start()

    add_up(0)

    for peer in peers:
        w_to_core(7, peer, 1 - c).wait_recv()
    for way in range(2):
        seed_onward_arrival(way).wait_recv()
    own_bias = jnp.broadcast_to(bias[:, cols(y)], (128, 256)).T
    own_bias = jnp.concatenate([own_bias] * 8, axis=1)
    pre[...] = own_bias + jnp.dot(
        wr_self[...].reshape(768, 256).T,
        x_self[...].reshape(768, 1024),
        preferred_element_type=F32,
    )
    cot_t[...] = cot[...].T.astype(F32)

    add_up(1)
    add_up(2)

    for peer in peers:
        w_to_core(8, peer, 1 - c).wait_recv()
    for part in range(3):
        weight = wr_a[part].reshape(256, 256).T
        for peer in peers:
            y_arrival(3 + part, x_a.at[part, peer], x_a.at[part, peer], peer).wait_recv()
        pre[...] += jnp.dot(
            weight, x_a[part].reshape(256, 1024), preferred_element_type=F32
        )

    def activate(b, _):
        rows = pl.ds(pl.multiple_of(b * 32, 32), 32)
        v = pre[rows, :]
        s = 1.0 / (1.0 + jnp.exp(-v))
        hid_t[rows, :] = (v * s).astype(BF)
        gp[rows, :] = (cot_t[rows, :] * (s * (1.0 + v * (1.0 - s)))).astype(BF)
        return 0

    lax.fori_loop(0, 8, activate, 0)

    def weigh(b, _):
        sources = [(x_self[b], 0, 192)]
        sources += [(x_a[part, b], 192 + 64 * part, 64) for part in range(3)]
        for source_rows, lo, n in sources:
            value = lax.dot_general(source_rows, gp[...], NT, preferred_element_type=F32)
            rows = pl.ds(pl.multiple_of(b * 384 + lo, 64), n)
            grad[0, rows, :] = value[:, :128]
            grad[1, rows, :] = value[:, 128:]
        return 0

    lax.fori_loop(0, 4, weigh, 0)
    ones = jnp.ones((16, 1024), BF)
    bias_parts[0] = lax.dot_general(ones, gp[...], NT, preferred_element_type=F32)[:8]

    def d_copy(kind, src, dst, to_sem, from_sem, device):
        return pltpu.make_async_remote_copy(
            src_ref=src,
            dst_ref=dst,
            send_sem=d_send.at[kind, to_sem],
            recv_sem=d_recv.at[kind, from_sem],
            device_id=device,
            device_id_type=MESH,
        )

    ahead = (1, 3, 2)

    def along_x(x2):
        return at(y, seed_id(z, x2, c))

    def along_z(z2):
        return at(y, seed_id(z2, x, c))

    core_copy = d_copy(0, grad.at[1 - c], core_in, 0, 0, other)
    core_bias = d_copy(1, bias_parts.at[0], bias_red.at[0], 0, 0, other)
    core_copy.start()
    core_bias.start()
    hid[...] = hid_t[...].T
    core_copy.wait_recv()
    core_bias.wait_recv()
    half[...] = (grad[c] + core_in[...]).reshape(4, 384, 128)
    bias_parts[1] = bias_parts[0] + bias_red[0]

    def piece(i, n):
        return pl.ds(pl.multiple_of(i * n, n), n)

    orders = ((x, along_x, z, along_z), (z, along_z, x, along_x))
    sent = [core_copy, core_bias]
    for k in ahead:
        for o, (mine, along, _, _) in enumerate(orders):
            to = (mine + k) % 4
            copy = d_copy(
                2 + o, half.at[pl.ds(2 * o, 2), piece(to, 96)], red2.at[o, mine], to, mine, along(to)
            )
            copy.start()
            sent.append(copy)
        to = (x + k) % 4
        copy = d_copy(4, bias_parts.at[1], bias_red.at[1 + x], to, x, along_x(to))
        copy.start()
        sent.append(copy)
    for o, (mine, along, _, _) in enumerate(orders):
        total = half[2 * o : 2 * o + 2, piece(mine, 96), :]
        for k in ahead:
            fr = (mine + k) % 4
            d_copy(
                2 + o, half.at[pl.ds(2 * o, 2), piece(fr, 96)], red2.at[o, fr], fr, fr, along(fr)
            ).wait_recv()
            total = total + red2[o, fr]
        part2[o] = total
    total = bias_parts[1]
    for k in ahead:
        fr = (x + k) % 4
        d_copy(4, bias_parts.at[1], bias_red.at[1 + fr], fr, fr, along_x(fr)).wait_recv()
        total = total + bias_red[1 + fr]
    bias_parts[2] = total

    for k in ahead:
        for o, (_, _, mine, along) in enumerate(orders):
            to = (mine + k) % 4
            copy = d_copy(
                5 + o, part2.at[o, :, piece(to, 24)], red3.at[o, mine], to, mine, along(to)
            )
            copy.start()
            sent.append(copy)
        to = (z + k) % 4
        copy = d_copy(7, bias_parts.at[2], bias_red.at[5 + z], to, z, along_z(to))
        copy.start()
        sent.append(copy)
    for o, (_, _, mine, along) in enumerate(orders):
        total = part2[o, :, piece(mine, 24), :]
        for k in ahead:
            fr = (mine + k) % 4
            d_copy(
                5 + o, part2.at[o, :, piece(fr, 24)], red3.at[o, fr], fr, fr, along(fr)
            ).wait_recv()
            total = total + red3[o, fr]
        part3[2 * o : 2 * o + 2] = total
    total = bias_parts[2]
    for k in ahead:
        fr = (z + k) % 4
        d_copy(7, bias_parts.at[2], bias_red.at[5 + fr], fr, fr, along_z(fr)).wait_recv()
        total = total + bias_red[5 + fr]
    bias_full[y] = total

    for k in ahead:
        to = (y + k) % 4
        copy = d_copy(8, part3.at[to], done.at[y], to, y, at(to, me))
        copy.start()
        sent.append(copy)
        copy = d_copy(9, bias_full.at[y], bias_full.at[y], to, y, at(to, me))
        copy.start()
        sent.append(copy)
    done[y] = part3[y]
    for k in ahead:
        fr = (y + k) % 4
        d_copy(8, part3.at[fr], done.at[fr], fr, fr, at(fr, me)).wait_recv()
        d_copy(9, bias_full.at[fr], bias_full.at[fr], fr, fr, at(fr, me)).wait_recv()

    def piece_of(z2, x2):
        return jnp.where(y < 2, 4 * x2 + z2, 4 * z2 + x2)

    def turned(i):
        dz, dx, _ = offset(i)
        return jnp.where(c == 1, -dx, dz), jnp.where(c == 1, dz, dx)

    def chip_copy(i, p):
        dz, dx = turned(i)
        return pltpu.make_async_remote_copy(
            src_ref=full.at[c, p],
            dst_ref=full.at[c, p],
            send_sem=chip_send.at[i],
            recv_sem=chip_recv.at[p],
            device_id=at(y, seed_id((z + dz + 4) % 4, (x + dx + 4) % 4, c)),
            device_id_type=MESH,
        )

    def core_share(core, p):
        return pltpu.make_async_remote_copy(
            src_ref=full.at[core, p],
            dst_ref=full.at[core, p],
            send_sem=core_send.at[p],
            recv_sem=core_recv.at[p],
            device_id=other,
            device_id_type=MESH,
        )

    mine = piece_of(z, x)
    full[c, mine] = done[...].reshape(96, 128).astype(BF)

    def spread(i, _):
        chip_copy(i, mine).start()
        return 0

    lax.fori_loop(0, 15, spread, 0)
    core_share(c, mine).start()

    def collect(i, _):
        dz, dx = turned(i)
        p = piece_of((z - dz + 4) % 4, (x - dx + 4) % 4)
        chip_copy(i, p).wait_recv()
        core_share(c, p).start()
        return 0

    lax.fori_loop(0, 15, collect, 0)

    def collect_core(p, _):
        core_share(1 - c, p).wait_recv()
        return 0

    lax.fori_loop(0, 16, collect_core, 0)

    for p in range(16):
        ref, row = (g_self, 24 * p) if p < 8 else (g_neigh, 24 * (p - 8))
        for core in range(2):
            value = full[core, p].astype(F32)
            for q in range(4):
                lane = q * 256 + core * 128
                ref[row : row + 24, lane : lane + 128] = value[q * 24 : (q + 1) * 24]
    for q in range(4):
        g_bias[:, q * 256 : (q + 1) * 256] = bias_full[q, 0:1, :]

    def left_done(i, _):
        chip_copy(i, mine).wait_send()
        return 0

    lax.fori_loop(0, 15, left_done, 0)

    def left_core(p, _):
        core_share(c, p).wait_send()
        return 0

    lax.fori_loop(0, 16, left_core, 0)
    for copy in sent:
        copy.wait_send()
    for peer in peers:
        for copy in w_copies(peer):
            copy.wait_send()
        w_to_core(7, peer, c).wait_send()
        w_to_core(8, peer, c).wait_send()
        for part in range(3):
            y_copy(3 + part, x_a.at[part, y], x_a.at[part, y], peer).wait_send()

    for k in range(2):
        seed_copy((up, down)[k]).wait_send()
        seed_onward(k).wait_send()

    def left(i, _):
        for part in range(3):
            row_copy(part, target(i), me).wait_send()
        return 0

    def left_whole(i, _):
        row_copy(3, target(i), me).wait_send()
        return 0

    lax.fori_loop(16, 31, left, 0)
    lax.fori_loop(0, 16, left_whole, 0)


def hand_over(*refs):
    for made, out in zip(refs[:4], refs[4:]):
        out[...] = made[...]


def local(node_feats, seed_feats, w_self, w_neigh, bias, send_list, nbr_slot, cotangent):
    vmem = pl.BlockSpec(memory_space=pltpu.VMEM)
    V, DMA = pltpu.VMEM, pltpu.SemaphoreType.DMA
    made = pl.pallas_call(
        kernel,
        out_shape=(
            jax.ShapeDtypeStruct((1024, 256), BF),
            jax.ShapeDtypeStruct((192, 1024), F32),
            jax.ShapeDtypeStruct((192, 1024), F32),
            jax.ShapeDtypeStruct((1, 1024), F32),
        ),
        in_specs=[vmem] * 8,
        out_specs=(vmem,) * 4,
        scratch_shapes=[
            V((3072, 256), BF),
            V((1024, 128), I32),
            V((128, 256), I32),
            V((32, 192, 256), BF),
            V((32, 192, 256), BF),
            V((32, 1024, 256), BF),
            V((192, 1024), F32),
            V((4, 192, 1024), BF),
            V((3, 4, 64, 1024), BF),
            V((4, 192, 256), BF),
            V((3, 4, 64, 256), BF),
            V((256, 1024), F32),
            V((256, 1024), F32),
            V((256, 1024), BF),
            V((256, 1024), BF),
            V((2, 1536, 128), F32),
            V((1536, 128), F32),
            V((4, 384, 128), F32),
            V((2, 4, 2, 96, 128), F32),
            V((2, 2, 96, 128), F32),
            V((2, 4, 2, 24, 128), F32),
            V((4, 24, 128), F32),
            V((4, 24, 128), F32),
            V((2, 16, 96, 128), BF),
            V((3, 8, 256), F32),
            V((9, 8, 256), F32),
            V((4, 8, 256), F32),
            DMA((4, 32)),
            DMA((4, 32)),
            DMA((9, 4)),
            DMA((9, 4)),
            DMA((10, 4)),
            DMA((10, 4)),
            DMA((16,)),
            DMA((16,)),
            DMA((16,)),
            DMA((16,)),
        ],
        compiler_params=pltpu.CompilerParams(
            collective_id=0, has_side_effects=True, vmem_limit_bytes=60 << 20
        ),
        name="sage_layer",
    )(
        node_feats.T,
        seed_feats,
        w_self,
        w_neigh.reshape(3, 64, 1024),
        bias.reshape(1, 1024),
        send_list.reshape(32, 256),
        nbr_slot.T,
        cotangent,
    )
    hidden, grad_self, grad_neigh, grad_bias = pl.pallas_call(
        hand_over,
        out_shape=tuple(jax.ShapeDtypeStruct(m.shape, m.dtype) for m in made),
        in_specs=[vmem] * 4,
        out_specs=(vmem,) * 4,
        name="hand_over",
    )(*made)
    return hidden, grad_self, grad_neigh, grad_bias.reshape(1024)


def solution(mesh):
    placed = (
        P("seed", "feat"),
        P("feat", "seed"),
        P("feat", None),
        P("feat", None),
        P(),
        P("seed", None, None),
        P("seed", None),
        P("seed", "feat"),
    )
    return jax.shard_map(
        local,
        mesh=mesh,
        in_specs=placed,
        out_specs=(P("seed", "feat"), P("feat", None), P("feat", None), P()),
        check_vma=False,
    )
```

time: 126 us -> 105 us (0.83)
  Pallas kernels: 115 us -> 104 us
  local copies, waits for them, and re-layouts: 10.1 us -> 0 us
    pallas_call x1, Pallas kernels: 115 us -> 101 us  [local(): pl.pallas_call(kernel, out_shape=(jax.ShapeDtypeStruct((1024, 256), BF),...]
    unnamed x12 -> x0, local copies, waits for them, and re-layouts: 9.17 us -> none
    pallas_call x0 -> x1, Pallas kernels: none -> 2.9 us  [local(): pl.pallas_call(hand_over, out_shape=tuple((jax.ShapeDtypeStruct(m.shape,...]
where the time goes in v2:
time: 105 us
  Pallas kernels  104 us (99%)
    pallas_call x1, Pallas kernels, local(): pl.pallas_call(kernel, out_shape=(jax.ShapeDtypeStruct((1024, 256), BF),...  101 us
    pallas_call x1, Pallas kernels, local(): pl.pallas_call(hand_over, out_shape=tuple((jax.ShapeDtypeStruct(m.shape,...  2.9 us

profile of v2, /device:TPU:1, one launch (start us, length us, event | category | flops | bytes accessed | tf_op | source)
XLA Modules:
  0.0 104.7 jit_solution(4722777660781860240)
XLA Ops:
  0.6 101.2 %sage_layer.1 = (bf16[1024,256]{1,0:T(8,128)(2,1)}, f32[192,1024]{1,0:T(8,128)}, f32[192,1024]{1,0:T(8,128)}, f32[1,1024]{1,0:T(1,128)}) custom-call(bf16[192,4096]{1,0:T(8,128)(2,1)} %bitcast.6, bf16[192,1024]{1,0:T(8,128)(2,1)} %seed.1, bf16[192,1024]{1,0:T(8,128)(2,1)} %w_self.1, bf16[3,64,1024]{2,1,0:T(8,128)(2,1)} %bitcast.7, f32[1,1024]{1,0:T(1,128)} %bitcast.10, ...), custom_call_target="tpu_custom_call" | custom-call | tf_op jit(solution)/shard_map/sage_layer/pallas_call | solution.py:583
  101.8 2.9 %hand_over.1 = (bf16[1024,256]{1,0:T(8,128)(2,1)}, f32[192,1024]{1,0:T(8,128)}, f32[192,1024]{1,0:T(8,128)}, f32[1,1024]{1,0:T(1,128)}) custom-call(bf16[1024,256]{1,0:T(8,128)(2,1)} %get-tuple-element.12.refs_0_, f32[192,1024]{1,0:T(8,128)} %get-tuple-element.13.refs_1_, f32[192,1024]{1,0:T(8,128)} %get-tuple-element.14.refs_2_, ...), custom_call_target="tpu_custom_call" | custom-call | tf_op jit(solution)/shard_map/hand_over/pallas_call | solution.py:646

commit v3 on v2

--- a/solution.py
+++ b/solution.py
@@ -31,13 +31,13 @@
 
 
 def kernel(
-    node, seed, w_self, w_neigh, bias, send_list, nbr, cot,
+    node, seed, w_self, w_neigh, bias_hbm, send_list_hbm, nbr_hbm, cot_hbm,
     hid, g_self, g_neigh, g_bias,
-    node_t, slots, groups, out_rows, in_rows, counts, acc, x_self, x_a, wr_self, wr_a,
+    node_t, send_list, nbr, bias, cot, slots, groups, out_rows, in_rows, counts, acc, x_self, x_a, wr_self, wr_a,
     pre, cot_t, hid_t, gp, grad, core_in, half, red2, part2, red3, part3, done, full,
     bias_parts, bias_red, bias_full,
     row_send, row_recv, y_send, y_recv, d_send, d_recv,
-    chip_send, chip_recv, core_send, core_recv,
+    chip_send, chip_recv, core_send, core_recv, load_sem,
 ):
     y = lax.axis_index("feat")
     me = lax.axis_index("seed")
@@ -76,25 +76,26 @@
             barrier, inc=1, device_id=at((y + k) % 4, me), device_id_type=MESH
         )
 
-    for j in range(16):
-        for q in range(3):
-            start = q * 1024 + j * 64
-            node_t[start : start + 64, :] = node[
-                q * 64 : (q + 1) * 64, j * 256 : (j + 1) * 256
+    def cols(peer):
+        return pl.ds(pl.multiple_of(peer * 256, 256), 256)
+
+    loads = [
+        pltpu.make_async_copy(src, dst, load_sem.at[k])
+        for k, (src, dst) in enumerate(
+            [(send_list_hbm, send_list)]
+            + [(node.at[:, pl.ds(256 * j, 256)], node_t.at[j]) for j in range(16)]
+            + [
+                (nbr_hbm, nbr),
+                (w_self.at[:, cols(y)], wr_self.at[y]),
+                (w_neigh.at[:, cols(y)], wr_a.at[y]),
+                (seed, x_self.at[y]),
+                (bias_hbm, bias),
+                (cot_hbm, cot),
             ]
-
-    slots[...] = jnp.concatenate(
-        [nbr[...], jnp.full((103, 1024), -1, I32)], axis=0
-    ).T
-    lane_group = lax.broadcasted_iota(I32, (128, 128), 1) // 32
-    for part in range(2):
-        line = slots[pl.ds(4 * part, 128, stride=8), :]
-        for k in (1, 2, 3):
-            moved = pltpu.roll(slots[pl.ds(4 * part + k, 128, stride=8), :], 32 * k, 1)
-            line = jnp.where(lane_group == k, moved, line)
-        groups[:, part * 128 : (part + 1) * 128] = line
-
-    pl.semaphore_wait(barrier, 34)
+        )
+    ]
+    for load in loads:
+        load.start()
 
     def y_copy(kind, src, dst, peer):
         return pltpu.make_async_remote_copy(
@@ -116,9 +117,6 @@
             device_id_type=MESH,
         )
 
-    def cols(peer):
-        return pl.ds(pl.multiple_of(peer * 256, 256), 256)
-
     def half_cols(peer, core):
         return pl.ds(pl.multiple_of(peer * 256 + core * 128, 128), 128)
 
@@ -134,7 +132,7 @@
         own = half_cols(peer, c)
         return (
             y_copy(0, w_self.at[:, own], wr_self.at[y, :, side], peer),
-            y_copy(1, w_neigh.at[:, :, own], wr_a.at[:, y, :, side], peer),
+            y_copy(1, w_neigh.at[:, own], wr_a.at[y, :, side], peer),
         )
 
     def seed_onward(way):
@@ -161,7 +159,7 @@
 
     def w_to_core(kind, peer, core):
         part = half_cols(0, core)
-        ref = wr_self.at[peer, :, part] if kind == 7 else wr_a.at[:, peer, :, part]
+        ref = (wr_self if kind == 7 else wr_a).at[peer, :, part]
         return pltpu.make_async_remote_copy(
             src_ref=ref,
             dst_ref=ref,
@@ -171,16 +169,6 @@
             device_id_type=MESH,
         )
 
-    for peer in (up, down):
-        seed_copy(peer).start()
-    for peer in peers:
-        for copy in w_copies(peer):
-            copy.start()
-    wr_self[y] = w_self[:, cols(y)]
-    for part in range(3):
-        wr_a[part, y] = w_neigh[part, :, cols(y)]
-    x_self[y] = seed[...]
-
     def row_copy(part, to, sender):
         rows = pl.ds(0, 192) if part == 3 else pl.ds(64 * part, 64)
         return pltpu.make_async_remote_copy(
@@ -198,11 +186,14 @@
     def one_hot(row):
         return jnp.where(ids == row, 1.0, 0.0).astype(BF)
 
+    def span(part):
+        return slice(0, 192) if part == 3 else slice(64 * part, 64 * part + 64)
+
     def gather(part, to):
         index = send_list[pl.ds(to, 1), :]
         block, chosen = index // 256, one_hot(index % 256)
         every = jnp.dot(
-            node_t[part * 1024 : (part + 1) * 1024, :], chosen, preferred_element_type=F32
+            node_t[:, span(part), :].reshape(1024, 256), chosen, preferred_element_type=F32
         )
         rows = jnp.zeros((64, 256), F32)
         for j in range(16):
@@ -224,9 +215,6 @@
                 found, axis=1
             ).astype(BF)
 
-    def span(part):
-        return slice(0, 192) if part == 3 else slice(64 * part, 64 * part + 64)
-
     def own_term(part):
         return lax.dot_general(
             out_rows[me, span(part), :], counts[me], NT, preferred_element_type=F32
@@ -287,8 +275,36 @@
         row_copy(2, target(i), me).start()
         return 0
 
+    for load in loads[:17]:
+        load.wait()
+    to = [target(k) for k in range(2)]
+    for k in range(2):
+        for part in range(3):
+            gather(part, to[k])
+    pl.semaphore_wait(barrier, 34)
+    for k in range(2):
+        row_copy(3, to[k], me).start()
+    for peer in (up, down):
+        seed_copy(peer).start()
+    for peer in peers:
+        for copy in w_copies(peer):
+            copy.start()
+
+    for load in loads[17:21]:
+        load.wait()
+    slots[...] = jnp.concatenate([nbr[...], jnp.full((103, 1024), -1, I32)], axis=0).T
+    lane_group = lax.broadcasted_iota(I32, (128, 128), 1) // 32
+    for part in range(2):
+        line = slots[pl.ds(4 * part, 128, stride=8), :]
+        for k in (1, 2, 3):
+            moved = pltpu.roll(slots[pl.ds(4 * part + k, 128, stride=8), :], 32 * k, 1)
+            line = jnp.where(lane_group == k, moved, line)
+        groups[:, part * 128 : (part + 1) * 128] = line
+
     acc[...] = jnp.zeros((192, 1024), F32)
-    lax.fori_loop(0, 8, early_step, 0)
+    lax.fori_loop(1, 8, early_step, 0)
+    count(0)
+    count(1)
     lax.fori_loop(0, 4, late_first, 0)
     for peer in (up, down):
         y_arrival(2, seed, x_self.at[peer], peer).wait_recv()
@@ -297,12 +313,16 @@
     for peer in peers:
         own = half_cols(peer, c)
         y_arrival(0, w_self.at[:, own], wr_self.at[peer, :, side], peer).wait_recv()
-        y_arrival(1, w_neigh.at[:, :, own], wr_a.at[:, peer, :, side], peer).wait_recv()
+        y_arrival(1, w_neigh.at[:, own], wr_a.at[peer, :, side], peer).wait_recv()
         w_to_core(7, peer, c).start()
         w_to_core(8, peer, c).start()
     lax.fori_loop(0, 4, late_rest, 0)
     lax.fori_loop(16, 31, late_last, 0)
 
+    def averaged_copy(part, peer):
+        ref = x_a.at[y, pl.ds(64 * part, 64)]
+        return y_copy(3 + part, ref, ref, peer)
+
     def add_up(part):
         rows = span(part)
         acc[rows, :] += own_term(part)
@@ -312,9 +332,9 @@
             return 0
 
         lax.fori_loop(0, 3, five, 0)
-        x_a[part, y] = (acc[rows, :] * (1.0 / 25.0)).astype(BF)
+        x_a[y, rows, :] = (acc[rows, :] * (1.0 / 25.0)).astype(BF)
         for peer in peers:
-            y_copy(3 + part, x_a.at[part, y], x_a.at[part, y], peer).start()
+            averaged_copy(part, peer).start()
 
     add_up(0)
 
@@ -322,6 +342,8 @@
         w_to_core(7, peer, 1 - c).wait_recv()
     for way in range(2):
         seed_onward_arrival(way).wait_recv()
+    for load in loads[21:]:
+        load.wait()
     own_bias = jnp.broadcast_to(bias[:, cols(y)], (128, 256)).T
     own_bias = jnp.concatenate([own_bias] * 8, axis=1)
     pre[...] = own_bias + jnp.dot(
@@ -337,11 +359,12 @@
     for peer in peers:
         w_to_core(8, peer, 1 - c).wait_recv()
     for part in range(3):
-        weight = wr_a[part].reshape(256, 256).T
+        weight = wr_a[:, span(part), :].reshape(256, 256).T
         for peer in peers:
-            y_arrival(3 + part, x_a.at[part, peer], x_a.at[part, peer], peer).wait_recv()
+            ref = x_a.at[peer, pl.ds(64 * part, 64)]
+            y_arrival(3 + part, ref, ref, peer).wait_recv()
         pre[...] += jnp.dot(
-            weight, x_a[part].reshape(256, 1024), preferred_element_type=F32
+            weight, x_a[:, span(part), :].reshape(256, 1024), preferred_element_type=F32
         )
 
     def activate(b, _):
@@ -354,20 +377,6 @@
 
     lax.fori_loop(0, 8, activate, 0)
 
-    def weigh(b, _):
-        sources = [(x_self[b], 0, 192)]
-        sources += [(x_a[part, b], 192 + 64 * part, 64) for part in range(3)]
-        for source_rows, lo, n in sources:
-            value = lax.dot_general(source_rows, gp[...], NT, preferred_element_type=F32)
-            rows = pl.ds(pl.multiple_of(b * 384 + lo, 64), n)
-            grad[0, rows, :] = value[:, :128]
-            grad[1, rows, :] = value[:, 128:]
-        return 0
-
-    lax.fori_loop(0, 4, weigh, 0)
-    ones = jnp.ones((16, 1024), BF)
-    bias_parts[0] = lax.dot_general(ones, gp[...], NT, preferred_element_type=F32)[:8]
-
     def d_copy(kind, src, dst, to_sem, from_sem, device):
         return pltpu.make_async_remote_copy(
             src_ref=src,
@@ -386,33 +395,55 @@
     def along_z(z2):
         return at(y, seed_id(z2, x, c))
 
-    core_copy = d_copy(0, grad.at[1 - c], core_in, 0, 0, other)
+    def core_rows(o):
+        return d_copy(
+            0, grad.at[1 - c, pl.ds(768 * o, 768)], core_in.at[pl.ds(768 * o, 768)], o, o, other
+        )
+
     core_bias = d_copy(1, bias_parts.at[0], bias_red.at[0], 0, 0, other)
-    core_copy.start()
+    sent = [core_rows(0), core_rows(1), core_bias]
+    for o in range(2):
+        for first, source_rows in ((0, x_self), (192, x_a)):
+            value = lax.dot_general(
+                source_rows[2 * o : 2 * o + 2].reshape(384, 1024),
+                gp[...],
+                NT,
+                preferred_element_type=F32,
+            )
+            for b in range(2):
+                row = (2 * o + b) * 384 + first
+                for core in range(2):
+                    grad[core, row : row + 192, :] = value[
+                        b * 192 : (b + 1) * 192, core * 128 : (core + 1) * 128
+                    ]
+        sent[o].start()
+    ones = jnp.ones((16, 1024), BF)
+    bias_parts[0] = lax.dot_general(ones, gp[...], NT, preferred_element_type=F32)[:8]
     core_bias.start()
-    hid[...] = hid_t[...].T
-    core_copy.wait_recv()
-    core_bias.wait_recv()
-    half[...] = (grad[c] + core_in[...]).reshape(4, 384, 128)
-    bias_parts[1] = bias_parts[0] + bias_red[0]
 
     def piece(i, n):
         return pl.ds(pl.multiple_of(i * n, n), n)
 
     orders = ((x, along_x, z, along_z), (z, along_z, x, along_x))
-    sent = [core_copy, core_bias]
-    for k in ahead:
-        for o, (mine, along, _, _) in enumerate(orders):
+    for o, (mine, along, _, _) in enumerate(orders):
+        sent[o].wait_recv()
+        rows = slice(768 * o, 768 * o + 768)
+        half[2 * o : 2 * o + 2] = (grad[c, rows, :] + core_in[rows, :]).reshape(2, 384, 128)
+        for k in ahead:
             to = (mine + k) % 4
             copy = d_copy(
                 2 + o, half.at[pl.ds(2 * o, 2), piece(to, 96)], red2.at[o, mine], to, mine, along(to)
             )
             copy.start()
             sent.append(copy)
+    core_bias.wait_recv()
+    bias_parts[1] = bias_parts[0] + bias_red[0]
+    for k in ahead:
         to = (x + k) % 4
         copy = d_copy(4, bias_parts.at[1], bias_red.at[1 + x], to, x, along_x(to))
         copy.start()
         sent.append(copy)
+    hid[...] = hid_t[...].T
     for o, (mine, along, _, _) in enumerate(orders):
         total = half[2 * o : 2 * o + 2, piece(mine, 96), :]
         for k in ahead:
@@ -553,7 +584,7 @@
         w_to_core(7, peer, c).wait_send()
         w_to_core(8, peer, c).wait_send()
         for part in range(3):
-            y_copy(3 + part, x_a.at[part, y], x_a.at[part, y], peer).wait_send()
+            averaged_copy(part, peer).wait_send()
 
     for k in range(2):
         seed_copy((up, down)[k]).wait_send()
@@ -573,8 +604,21 @@
 
 
 def hand_over(*refs):
-    for made, out in zip(refs[:4], refs[4:]):
-        out[...] = made[...]
+    sem_in, sem_out = refs[12:]
+    inward, outward = [], []
+    for made, out, held, parts in zip(refs[:4], refs[4:8], refs[8:12], (2, 2, 2, 1)):
+        rows = made.shape[0] // parts
+        for part in range(parts):
+            k, span = len(inward), pl.ds(part * rows, rows)
+            inward.append(pltpu.make_async_copy(made.at[span], held.at[span], sem_in.at[k]))
+            outward.append(pltpu.make_async_copy(held.at[span], out.at[span], sem_out.at[k]))
+    for copy in inward:
+        copy.start()
+    for there, back in zip(inward, outward):
+        there.wait()
+        back.start()
+    for copy in outward:
+        copy.wait()
 
 
 def local(node_feats, seed_feats, w_self, w_neigh, bias, send_list, nbr_slot, cotangent):
@@ -588,10 +632,14 @@
             jax.ShapeDtypeStruct((192, 1024), F32),
             jax.ShapeDtypeStruct((1, 1024), F32),
         ),
-        in_specs=[vmem] * 8,
+        in_specs=[pl.BlockSpec(memory_space=pl.ANY)] * 8,
         out_specs=(vmem,) * 4,
         scratch_shapes=[
-            V((3072, 256), BF),
+            V((16, 192, 256), BF),
+            V((32, 256), I32),
+            V((25, 1024), I32),
+            V((1, 1024), F32),
+            V((1024, 256), BF),
             V((1024, 128), I32),
             V((128, 256), I32),
             V((32, 192, 256), BF),
@@ -599,9 +647,9 @@
             V((32, 1024, 256), BF),
             V((192, 1024), F32),
             V((4, 192, 1024), BF),
-            V((3, 4, 64, 1024), BF),
+            V((4, 192, 1024), BF),
             V((4, 192, 256), BF),
-            V((3, 4, 64, 256), BF),
+            V((4, 192, 256), BF),
             V((256, 1024), F32),
             V((256, 1024), F32),
             V((256, 1024), BF),
@@ -628,6 +676,7 @@
             DMA((16,)),
             DMA((16,)),
             DMA((16,)),
+            DMA((23,)),
         ],
         compiler_params=pltpu.CompilerParams(
             collective_id=0, has_side_effects=True, vmem_limit_bytes=60 << 20
@@ -637,7 +686,7 @@
         node_feats.T,
         seed_feats,
         w_self,
-        w_neigh.reshape(3, 64, 1024),
+        w_neigh,
         bias.reshape(1, 1024),
         send_list.reshape(32, 256),
         nbr_slot.T,
@@ -646,8 +695,9 @@
     hidden, grad_self, grad_neigh, grad_bias = pl.pallas_call(
         hand_over,
         out_shape=tuple(jax.ShapeDtypeStruct(m.shape, m.dtype) for m in made),
-        in_specs=[vmem] * 4,
-        out_specs=(vmem,) * 4,
+        in_specs=[pl.BlockSpec(memory_space=pl.ANY)] * 4,
+        out_specs=(pl.BlockSpec(memory_space=pl.ANY),) * 4,
+        scratch_shapes=[V(m.shape, m.dtype) for m in made] + [DMA((7,)), DMA((7,))],
         name="hand_over",
     )(*made)
     return hidden, grad_self, grad_neigh, grad_bias.reshape(1024)

time: 105 us -> 97.8 us (0.931)
  Pallas kernels: 104 us -> 97 us
    pallas_call x1, Pallas kernels: 101 us -> 94.6 us  [local(): pl.pallas_call(kernel, out_shape=(jax.ShapeDtypeStruct((1024, 256), BF),...]
where the time goes in v3:
time: 97.8 us; the launch traced here: 97.6 us
  Pallas kernels  97 us (99%)
    pallas_call x1, Pallas kernels, local(): pl.pallas_call(kernel, out_shape=(jax.ShapeDtypeStruct((1024, 256), BF),...  94.6 us
    pallas_call x1, Pallas kernels, local(): pl.pallas_call(hand_over, out_shape=tuple((jax.ShapeDtypeStruct(m.shape,...  2.41 us

profile of v3, /device:TPU:1, one launch (start us, length us, event | category | flops | bytes accessed | tf_op | source)
XLA Modules:
  0.0 97.6 jit_solution(1636335343359552210)
XLA Ops:
  0.6 94.6 %sage_layer.1 = (bf16[1024,256]{1,0:T(8,128)(2,1)}, f32[192,1024]{1,0:T(8,128)}, f32[192,1024]{1,0:T(8,128)}, f32[1,1024]{1,0:T(1,128)}) custom-call(bf16[192,4096]{1,0:T(8,128)(2,1)} %bitcast.5, bf16[192,1024]{1,0:T(8,128)(2,1)} %seed.1, bf16[192,1024]{1,0:T(8,128)(2,1)} %w_self.1, bf16[192,1024]{1,0:T(8,128)(2,1)} %w_neigh.1, f32[1,1024]{1,0:T(1,128)} %bitcast.8, ...), custom_call_target="tpu_custom_call" | custom-call | tf_op jit(solution)/shard_map/sage_layer/pallas_call | solution.py:627
  95.2 2.4 %hand_over.1 = (bf16[1024,256]{1,0:T(8,128)(2,1)}, f32[192,1024]{1,0:T(8,128)}, f32[192,1024]{1,0:T(8,128)}, f32[1,1024]{1,0:T(1,128)}) custom-call(bf16[1024,256]{1,0:T(8,128)(2,1)} %get-tuple-element.12.refs_0_, f32[192,1024]{1,0:T(8,128)} %get-tuple-element.13.refs_1_, f32[192,1024]{1,0:T(8,128)} %get-tuple-element.14.refs_2_, ...), custom_call_target="tpu_custom_call" | custom-call | tf_op jit(solution)/shard_map/hand_over/pallas_call | solution.py:695

commit v4 on v3

--- a/solution.py
+++ b/solution.py
@@ -32,12 +32,12 @@
 
 def kernel(
     node, seed, w_self, w_neigh, bias_hbm, send_list_hbm, nbr_hbm, cot_hbm,
-    hid, g_self, g_neigh, g_bias,
+    hid_hbm, full_hbm, g_bias,
     node_t, send_list, nbr, bias, cot, slots, groups, out_rows, in_rows, counts, acc, x_self, x_a, wr_self, wr_a,
-    pre, cot_t, hid_t, gp, grad, core_in, half, red2, part2, red3, part3, done, full,
+    pre, cot_t, hid_t, hid, gp, grad, core_in, half, red2, part2, red3, full,
     bias_parts, bias_red, bias_full,
     row_send, row_recv, y_send, y_recv, d_send, d_recv,
-    chip_send, chip_recv, core_send, core_recv, load_sem,
+    chip_send, chip_recv, core_send, core_recv, load_sem, out_sem, keep_send, keep_recv,
 ):
     y = lax.axis_index("feat")
     me = lax.axis_index("seed")
@@ -75,6 +75,11 @@
         pl.semaphore_signal(
             barrier, inc=1, device_id=at((y + k) % 4, me), device_id_type=MESH
         )
+        for turn in (1, 2, 3):
+            for seed_index in (seed_id((z + turn) % 4, x, c), seed_id(z, (x + turn) % 4, c)):
+                pl.semaphore_signal(
+                    barrier, inc=1, device_id=at((y + k) % 4, seed_index), device_id_type=MESH
+                )
 
     def cols(peer):
         return pl.ds(pl.multiple_of(peer * 256, 256), 256)
@@ -281,7 +286,7 @@
     for k in range(2):
         for part in range(3):
             gather(part, to[k])
-    pl.semaphore_wait(barrier, 34)
+    pl.semaphore_wait(barrier, 52)
     for k in range(2):
         row_copy(3, to[k], me).start()
     for peer in (up, down):
@@ -319,9 +324,18 @@
     lax.fori_loop(0, 4, late_rest, 0)
     lax.fori_loop(16, 31, late_last, 0)
 
+    def averaged_ref(part, owner):
+        if part < 2:
+            return x_a.at[owner, pl.ds(64 * part, 64)]
+        return x_a.at[owner, pl.ds(128, 64), pl.ds(512 * (part - 2), 512)]
+
     def averaged_copy(part, peer):
-        ref = x_a.at[y, pl.ds(64 * part, 64)]
-        return y_copy(3 + part, ref, ref, peer)
+        ref = averaged_ref(part, y)
+        return y_copy((3, 4, 5, 9)[part], ref, ref, peer)
+
+    def averaged_arrival(part, peer):
+        ref = averaged_ref(part, peer)
+        return y_arrival((3, 4, 5, 9)[part], ref, ref, peer)
 
     def add_up(part):
         rows = span(part)
@@ -333,8 +347,9 @@
 
         lax.fori_loop(0, 3, five, 0)
         x_a[y, rows, :] = (acc[rows, :] * (1.0 / 25.0)).astype(BF)
-        for peer in peers:
-            averaged_copy(part, peer).start()
+        for piece in (part,) if part < 2 else (2, 3):
+            for peer in peers:
+                averaged_copy(piece, peer).start()
 
     add_up(0)
 
@@ -358,24 +373,32 @@
 
     for peer in peers:
         w_to_core(8, peer, 1 - c).wait_recv()
-    for part in range(3):
+    for part in range(2):
         weight = wr_a[:, span(part), :].reshape(256, 256).T
         for peer in peers:
-            ref = x_a.at[peer, pl.ds(64 * part, 64)]
-            y_arrival(3 + part, ref, ref, peer).wait_recv()
+            averaged_arrival(part, peer).wait_recv()
         pre[...] += jnp.dot(
             weight, x_a[:, span(part), :].reshape(256, 1024), preferred_element_type=F32
         )
 
-    def activate(b, _):
-        rows = pl.ds(pl.multiple_of(b * 32, 32), 32)
-        v = pre[rows, :]
-        s = 1.0 / (1.0 + jnp.exp(-v))
-        hid_t[rows, :] = (v * s).astype(BF)
-        gp[rows, :] = (cot_t[rows, :] * (s * (1.0 + v * (1.0 - s)))).astype(BF)
-        return 0
-
-    lax.fori_loop(0, 8, activate, 0)
+    weight = wr_a[:, span(2), :].reshape(256, 256).T
+    for h in range(2):
+        lanes = slice(512 * h, 512 * h + 512)
+        for peer in peers:
+            averaged_arrival(2 + h, peer).wait_recv()
+        pre[:, lanes] += jnp.dot(
+            weight, x_a[:, span(2), lanes].reshape(256, 512), preferred_element_type=F32
+        )
+
+        def activate(b, _):
+            rows = pl.ds(pl.multiple_of(b * 64, 64), 64)
+            v = pre[rows, lanes]
+            s = 1.0 / (1.0 + jnp.exp(-v))
+            hid_t[rows, lanes] = (v * s).astype(BF)
+            gp[rows, lanes] = (cot_t[rows, lanes] * (s * (1.0 + v * (1.0 - s)))).astype(BF)
+            return 0
+
+        lax.fori_loop(0, 4, activate, 0)
 
     def d_copy(kind, src, dst, to_sem, from_sem, device):
         return pltpu.make_async_remote_copy(
@@ -444,6 +467,33 @@
         copy.start()
         sent.append(copy)
     hid[...] = hid_t[...].T
+    hid_out = pltpu.make_async_copy(hid, hid_hbm, out_sem.at[32])
+    hid_out.start()
+
+    for peer in peers:
+        for copy in w_copies(peer):
+            copy.wait_send()
+        w_to_core(7, peer, c).wait_send()
+        w_to_core(8, peer, c).wait_send()
+        for part in range(4):
+            averaged_copy(part, peer).wait_send()
+
+    for k in range(2):
+        seed_copy((up, down)[k]).wait_send()
+        seed_onward(k).wait_send()
+
+    def left(i, _):
+        for part in range(3):
+            row_copy(part, target(i), me).wait_send()
+        return 0
+
+    def left_whole(i, _):
+        row_copy(3, target(i), me).wait_send()
+        return 0
+
+    lax.fori_loop(16, 31, left, 0)
+    lax.fori_loop(0, 16, left_whole, 0)
+
     for o, (mine, along, _, _) in enumerate(orders):
         total = half[2 * o : 2 * o + 2, piece(mine, 96), :]
         for k in ahead:
@@ -460,108 +510,126 @@
         total = total + bias_red[1 + fr]
     bias_parts[2] = total
 
+    def keep(o, r, k):
+        mine = orders[o][2]
+        j = (mine + k) % 4
+        feat = 2 * o + r
+        return pltpu.make_async_remote_copy(
+            src_ref=part2.at[o, r, piece(j, 24)],
+            dst_ref=red3.at[y, mine],
+            send_sem=keep_send.at[feat, j],
+            recv_sem=keep_recv.at[y, mine],
+            device_id=at(feat, seed_id(j, x, c) if o == 0 else seed_id(z, j, c)),
+            device_id_type=MESH,
+        )
+
+    def each_kept(act):
+        for k in (2, 1, 3, 0):
+            for r in range(2):
+                for o in range(2):
+                    if k:
+                        act(keep(o, r, k))
+                    else:
+
+                        @pl.when(y != 2 * o + r)
+                        def _():
+                            act(keep(o, r, 0))
+
+    each_kept(lambda copy: copy.start())
     for k in ahead:
-        for o, (_, _, mine, along) in enumerate(orders):
-            to = (mine + k) % 4
-            copy = d_copy(
-                5 + o, part2.at[o, :, piece(to, 24)], red3.at[o, mine], to, mine, along(to)
-            )
-            copy.start()
-            sent.append(copy)
         to = (z + k) % 4
         copy = d_copy(7, bias_parts.at[2], bias_red.at[5 + z], to, z, along_z(to))
         copy.start()
         sent.append(copy)
-    for o, (_, _, mine, along) in enumerate(orders):
-        total = part2[o, :, piece(mine, 24), :]
-        for k in ahead:
-            fr = (mine + k) % 4
-            d_copy(
-                5 + o, part2.at[o, :, piece(fr, 24)], red3.at[o, fr], fr, fr, along(fr)
-            ).wait_recv()
-            total = total + red3[o, fr]
-        part3[2 * o : 2 * o + 2] = total
+    j0 = jnp.where(y < 2, z, x)
+    red3[y, j0] = part2[y // 2, y % 2, piece(j0, 24), :]
+    for ky in range(4):
+        for kj in range(4):
+            if ky or kj:
+                fr_y, fr_j = (y + ky) % 4, (j0 + kj) % 4
+                pltpu.make_async_remote_copy(
+                    src_ref=red3.at[fr_y, fr_j],
+                    dst_ref=red3.at[fr_y, fr_j],
+                    send_sem=keep_send.at[fr_y, fr_j],
+                    recv_sem=keep_recv.at[fr_y, fr_j],
+                    device_id=other,
+                    device_id_type=MESH,
+                ).wait_recv()
+    done = red3[:, 0] + red3[:, 1] + red3[:, 2] + red3[:, 3]
+
+    def piece_of(z2, x2):
+        return jnp.where(y < 2, 4 * x2 + z2, 4 * z2 + x2)
+
+    def turned(i):
+        dz, dx, _ = offset(i)
+        return jnp.where(c == 1, -dx, dz), jnp.where(c == 1, dz, dx)
+
+    def chip_copy(i, p):
+        dz, dx = turned(i)
+        return pltpu.make_async_remote_copy(
+            src_ref=full.at[c, p],
+            dst_ref=full.at[c, p],
+            send_sem=chip_send.at[i],
+            recv_sem=chip_recv.at[p],
+            device_id=at(y, seed_id((z + dz + 4) % 4, (x + dx + 4) % 4, c)),
+            device_id_type=MESH,
+        )
+
+    def core_share(core, p):
+        return pltpu.make_async_remote_copy(
+            src_ref=full.at[core, p],
+            dst_ref=full.at[core, p],
+            send_sem=core_send.at[p],
+            recv_sem=core_recv.at[p],
+            device_id=other,
+            device_id_type=MESH,
+        )
+
+    def piece_out(core, p):
+        return pltpu.make_async_copy(
+            full.at[core, p], full_hbm.at[core, p], out_sem.at[16 * core + p]
+        )
+
+    mine = piece_of(z, x)
+    full[c, mine] = done.reshape(96, 128).astype(BF)
+
+    for i in range(15):
+        chip_copy(i, mine).start()
+    core_share(c, mine).start()
+    piece_out(c, mine).start()
+
     total = bias_parts[2]
     for k in ahead:
         fr = (z + k) % 4
         d_copy(7, bias_parts.at[2], bias_red.at[5 + fr], fr, fr, along_z(fr)).wait_recv()
         total = total + bias_red[5 + fr]
     bias_full[y] = total
-
     for k in ahead:
         to = (y + k) % 4
-        copy = d_copy(8, part3.at[to], done.at[y], to, y, at(to, me))
-        copy.start()
-        sent.append(copy)
         copy = d_copy(9, bias_full.at[y], bias_full.at[y], to, y, at(to, me))
         copy.start()
         sent.append(copy)
-    done[y] = part3[y]
-    for k in ahead:
-        fr = (y + k) % 4
-        d_copy(8, part3.at[fr], done.at[fr], fr, fr, at(fr, me)).wait_recv()
-        d_copy(9, bias_full.at[fr], bias_full.at[fr], fr, fr, at(fr, me)).wait_recv()
-
-    def piece_of(z2, x2):
-        return jnp.where(y < 2, 4 * x2 + z2, 4 * z2 + x2)
-
-    def turned(i):
-        dz, dx, _ = offset(i)
-        return jnp.where(c == 1, -dx, dz), jnp.where(c == 1, dz, dx)
-
-    def chip_copy(i, p):
-        dz, dx = turned(i)
-        return pltpu.make_async_remote_copy(
-            src_ref=full.at[c, p],
-            dst_ref=full.at[c, p],
-            send_sem=chip_send.at[i],
-            recv_sem=chip_recv.at[p],
-            device_id=at(y, seed_id((z + dz + 4) % 4, (x + dx + 4) % 4, c)),
-            device_id_type=MESH,
-        )
-
-    def core_share(core, p):
-        return pltpu.make_async_remote_copy(
-            src_ref=full.at[core, p],
-            dst_ref=full.at[core, p],
-            send_sem=core_send.at[p],
-            recv_sem=core_recv.at[p],
-            device_id=other,
-            device_id_type=MESH,
-        )
-
-    mine = piece_of(z, x)
-    full[c, mine] = done[...].reshape(96, 128).astype(BF)
-
-    def spread(i, _):
-        chip_copy(i, mine).start()
-        return 0
-
-    lax.fori_loop(0, 15, spread, 0)
-    core_share(c, mine).start()
 
     def collect(i, _):
         dz, dx = turned(i)
         p = piece_of((z - dz + 4) % 4, (x - dx + 4) % 4)
         chip_copy(i, p).wait_recv()
         core_share(c, p).start()
+        piece_out(c, p).start()
         return 0
 
     lax.fori_loop(0, 15, collect, 0)
 
     def collect_core(p, _):
         core_share(1 - c, p).wait_recv()
+        piece_out(1 - c, p).start()
         return 0
 
     lax.fori_loop(0, 16, collect_core, 0)
 
-    for p in range(16):
-        ref, row = (g_self, 24 * p) if p < 8 else (g_neigh, 24 * (p - 8))
-        for core in range(2):
-            value = full[core, p].astype(F32)
-            for q in range(4):
-                lane = q * 256 + core * 128
-                ref[row : row + 24, lane : lane + 128] = value[q * 24 : (q + 1) * 24]
+    for k in ahead:
+        fr = (y + k) % 4
+        d_copy(9, bias_full.at[fr], bias_full.at[fr], fr, fr, at(fr, me)).wait_recv()
     for q in range(4):
         g_bias[:, q * 256 : (q + 1) * 256] = bias_full[q, 0:1, :]
 
@@ -573,67 +641,78 @@
 
     def left_core(p, _):
         core_share(c, p).wait_send()
+        piece_out(0, p).wait()
+        piece_out(1, p).wait()
         return 0
 
     lax.fori_loop(0, 16, left_core, 0)
+    each_kept(lambda copy: copy.wait_send())
+    hid_out.wait()
     for copy in sent:
         copy.wait_send()
-    for peer in peers:
-        for copy in w_copies(peer):
-            copy.wait_send()
-        w_to_core(7, peer, c).wait_send()
-        w_to_core(8, peer, c).wait_send()
-        for part in range(3):
-            averaged_copy(part, peer).wait_send()
-
-    for k in range(2):
-        seed_copy((up, down)[k]).wait_send()
-        seed_onward(k).wait_send()
-
-    def left(i, _):
-        for part in range(3):
-            row_copy(part, target(i), me).wait_send()
-        return 0
-
-    def left_whole(i, _):
-        row_copy(3, target(i), me).wait_send()
-        return 0
-
-    lax.fori_loop(16, 31, left, 0)
-    lax.fori_loop(0, 16, left_whole, 0)
-
-
-def hand_over(*refs):
-    sem_in, sem_out = refs[12:]
-    inward, outward = [], []
-    for made, out, held, parts in zip(refs[:4], refs[4:8], refs[8:12], (2, 2, 2, 1)):
-        rows = made.shape[0] // parts
-        for part in range(parts):
-            k, span = len(inward), pl.ds(part * rows, rows)
-            inward.append(pltpu.make_async_copy(made.at[span], held.at[span], sem_in.at[k]))
-            outward.append(pltpu.make_async_copy(held.at[span], out.at[span], sem_out.at[k]))
+
+
+def hand_over(
+    hid_in, pieces_in, bias_in, hid, g_self, g_neigh, g_bias,
+    hid_held, pieces, grads, bias_held, sem_in, sem_out,
+):
+    def quarter(i):
+        return pl.ds(4 * i, 4)
+
+    halves = [pl.ds(512 * h, 512) for h in range(2)]
+    inward = [
+        pltpu.make_async_copy(pieces_in.at[:, quarter(i)], pieces.at[:, quarter(i)], sem_in.at[i])
+        for i in range(4)
+    ]
+    inward += [
+        pltpu.make_async_copy(hid_in.at[h], hid_held.at[h], sem_in.at[4 + k])
+        for k, h in enumerate(halves)
+    ]
+    inward += [pltpu.make_async_copy(bias_in, bias_held, sem_in.at[6])]
+    outward = [
+        pltpu.make_async_copy(
+            grads.at[pl.ds(96 * i, 96)],
+            (g_self, g_neigh)[i // 2].at[pl.ds(96 * (i % 2), 96)],
+            sem_out.at[i],
+        )
+        for i in range(4)
+    ]
+    outward += [
+        pltpu.make_async_copy(hid_held.at[h], hid.at[h], sem_out.at[4 + k])
+        for k, h in enumerate(halves)
+    ]
+    outward += [pltpu.make_async_copy(bias_held, g_bias, sem_out.at[6])]
     for copy in inward:
         copy.start()
-    for there, back in zip(inward, outward):
-        there.wait()
-        back.start()
+    for i in (0, 1, 2, 3, 4, 5, 6):
+        inward[i].wait()
+        if i < 4:
+            for p in range(4 * i, 4 * i + 4):
+                for core in range(2):
+                    value = pieces[core, p].astype(F32)
+                    for q in range(4):
+                        lane = q * 256 + core * 128
+                        grads[24 * p : 24 * p + 24, lane : lane + 128] = value[
+                            24 * q : 24 * q + 24
+                        ]
+        outward[i].start()
     for copy in outward:
         copy.wait()
 
 
 def local(node_feats, seed_feats, w_self, w_neigh, bias, send_list, nbr_slot, cotangent):
     vmem = pl.BlockSpec(memory_space=pltpu.VMEM)
+    anywhere = pl.BlockSpec(memory_space=pl.ANY)
     V, DMA = pltpu.VMEM, pltpu.SemaphoreType.DMA
     made = pl.pallas_call(
         kernel,
         out_shape=(
             jax.ShapeDtypeStruct((1024, 256), BF),
-            jax.ShapeDtypeStruct((192, 1024), F32),
-            jax.ShapeDtypeStruct((192, 1024), F32),
+            jax.ShapeDtypeStruct((2, 16, 96, 128), BF),
             jax.ShapeDtypeStruct((1, 1024), F32),
         ),
-        in_specs=[pl.BlockSpec(memory_space=pl.ANY)] * 8,
-        out_specs=(vmem,) * 4,
+        in_specs=[anywhere] * 8,
+        out_specs=(anywhere, anywhere, vmem),
         scratch_shapes=[
             V((16, 192, 256), BF),
             V((32, 256), I32),
@@ -653,23 +732,22 @@
             V((256, 1024), F32),
             V((256, 1024), F32),
             V((256, 1024), BF),
+            V((1024, 256), BF),
             V((256, 1024), BF),
             V((2, 1536, 128), F32),
             V((1536, 128), F32),
             V((4, 384, 128), F32),
             V((2, 4, 2, 96, 128), F32),
             V((2, 2, 96, 128), F32),
-            V((2, 4, 2, 24, 128), F32),
-            V((4, 24, 128), F32),
-            V((4, 24, 128), F32),
+            V((4, 4, 24, 128), F32),
             V((2, 16, 96, 128), BF),
             V((3, 8, 256), F32),
             V((9, 8, 256), F32),
             V((4, 8, 256), F32),
             DMA((4, 32)),
             DMA((4, 32)),
-            DMA((9, 4)),
-            DMA((9, 4)),
+            DMA((10, 4)),
+            DMA((10, 4)),
             DMA((10, 4)),
             DMA((10, 4)),
             DMA((16,)),
@@ -677,6 +755,9 @@
             DMA((16,)),
             DMA((16,)),
             DMA((23,)),
+            DMA((33,)),
+            DMA((4, 4)),
+            DMA((4, 4)),
         ],
         compiler_params=pltpu.CompilerParams(
             collective_id=0, has_side_effects=True, vmem_limit_bytes=60 << 20
@@ -694,10 +775,22 @@
     )
     hidden, grad_self, grad_neigh, grad_bias = pl.pallas_call(
         hand_over,
-        out_shape=tuple(jax.ShapeDtypeStruct(m.shape, m.dtype) for m in made),
-        in_specs=[pl.BlockSpec(memory_space=pl.ANY)] * 4,
-        out_specs=(pl.BlockSpec(memory_space=pl.ANY),) * 4,
-        scratch_shapes=[V(m.shape, m.dtype) for m in made] + [DMA((7,)), DMA((7,))],
+        out_shape=(
+            jax.ShapeDtypeStruct((1024, 256), BF),
+            jax.ShapeDtypeStruct((192, 1024), F32),
+            jax.ShapeDtypeStruct((192, 1024), F32),
+            jax.ShapeDtypeStruct((1, 1024), F32),
+        ),
+        in_specs=[anywhere] * 3,
+        out_specs=(anywhere,) * 4,
+        scratch_shapes=[
+            V((1024, 256), BF),
+            V((2, 16, 96, 128), BF),
+            V((384, 1024), F32),
+            V((1, 1024), F32),
+            DMA((7,)),
+            DMA((7,)),
+        ],
         name="hand_over",
     )(*made)
     return hidden, grad_self, grad_neigh, grad_bias.reshape(1024)

time: 97.8 us -> 96.8 us (0.990)
  Pallas kernels: 97 us -> 96 us
where the time goes in v4:
time: 96.8 us; the launch traced here: 96.6 us
  Pallas kernels  96 us (99%)
    pallas_call x1, Pallas kernels, local(): pl.pallas_call(kernel, out_shape=(jax.ShapeDtypeStruct((1024, 256), BF),...  93.6 us
    pallas_call x1, Pallas kernels, local(): pl.pallas_call(hand_over, out_shape=(jax.ShapeDtypeStruct((1024, 256), BF...  2.38 us

profile of v4, /device:TPU:1, one launch (start us, length us, event | category | flops | bytes accessed | tf_op | source)
XLA Modules:
  0.0 96.6 jit_solution(18361025827788167715)
XLA Ops:
  0.6 93.6 %sage_layer.1 = (bf16[1024,256]{1,0:T(8,128)(2,1)}, bf16[2,16,96,128]{3,2,1,0:T(8,128)(2,1)}, f32[1,1024]{1,0:T(1,128)}) custom-call(bf16[192,4096]{1,0:T(8,128)(2,1)} %bitcast.5, bf16[192,1024]{1,0:T(8,128)(2,1)} %seed.1, bf16[192,1024]{1,0:T(8,128)(2,1)} %w_self.1, bf16[192,1024]{1,0:T(8,128)(2,1)} %w_neigh.1, f32[1,1024]{1,0:T(1,128)} %bitcast.8, ...), custom_call_target="tpu_custom_call" | custom-call | tf_op jit(solution)/shard_map/sage_layer/pallas_call | solution.py:707
  94.2 2.4 %hand_over.1 = (bf16[1024,256]{1,0:T(8,128)(2,1)}, f32[192,1024]{1,0:T(8,128)}, f32[192,1024]{1,0:T(8,128)}, f32[1,1024]{1,0:T(1,128)}) custom-call(bf16[1024,256]{1,0:T(8,128)(2,1)} %get-tuple-element.11.hid_in, bf16[2,16,96,128]{3,2,1,0:T(8,128)(2,1)} %get-tuple-element.12.pieces_in, f32[1,1024]{1,0:T(1,128)} %get-tuple-element.13.bias_in), custom_call_target="tpu_custom_call" | custom-call | tf_op jit(solution)/shard_map/hand_over/pallas_call | solution.py:776

commit v5 on v4

--- a/solution.py
+++ b/solution.py
@@ -348,7 +348,7 @@
         lax.fori_loop(0, 3, five, 0)
         x_a[y, rows, :] = (acc[rows, :] * (1.0 / 25.0)).astype(BF)
         for piece in (part,) if part < 2 else (2, 3):
-            for peer in peers:
+            for peer in (across, up, down):
                 averaged_copy(piece, peer).start()
 
     add_up(0)
@@ -410,7 +410,7 @@
             device_id_type=MESH,
         )
 
-    ahead = (1, 3, 2)
+    ahead = (2, 1, 3)
 
     def along_x(x2):
         return at(y, seed_id(z, x2, c))

time: 96.8 us -> 95.8 us (0.990)
  Pallas kernels: 96 us -> 95 us
    pallas_call x1, Pallas kernels: 93.6 us -> 92.6 us  [local(): pl.pallas_call(kernel, out_shape=(jax.ShapeDtypeStruct((1024, 256), BF),...]
where the time goes in v5:
time: 95.8 us; the launch traced here: 95.7 us
  Pallas kernels  95 us (99%)
    pallas_call x1, Pallas kernels, local(): pl.pallas_call(kernel, out_shape=(jax.ShapeDtypeStruct((1024, 256), BF),...  92.6 us
    pallas_call x1, Pallas kernels, local(): pl.pallas_call(hand_over, out_shape=(jax.ShapeDtypeStruct((1024, 256), BF...  2.38 us

profile of v5, /device:TPU:1, one launch (start us, length us, event | category | flops | bytes accessed | tf_op | source)
XLA Modules:
  0.0 95.7 jit_solution(3325088192303955470)
XLA Ops:
  0.6 92.6 %sage_layer.1 = (bf16[1024,256]{1,0:T(8,128)(2,1)}, bf16[2,16,96,128]{3,2,1,0:T(8,128)(2,1)}, f32[1,1024]{1,0:T(1,128)}) custom-call(bf16[192,4096]{1,0:T(8,128)(2,1)} %bitcast.5, bf16[192,1024]{1,0:T(8,128)(2,1)} %seed.1, bf16[192,1024]{1,0:T(8,128)(2,1)} %w_self.1, bf16[192,1024]{1,0:T(8,128)(2,1)} %w_neigh.1, f32[1,1024]{1,0:T(1,128)} %bitcast.8, ...), custom_call_target="tpu_custom_call" | custom-call | tf_op jit(solution)/shard_map/sage_layer/pallas_call | solution.py:707
  93.3 2.4 %hand_over.1 = (bf16[1024,256]{1,0:T(8,128)(2,1)}, f32[192,1024]{1,0:T(8,128)}, f32[192,1024]{1,0:T(8,128)}, f32[1,1024]{1,0:T(1,128)}) custom-call(bf16[1024,256]{1,0:T(8,128)(2,1)} %get-tuple-element.11.hid_in, bf16[2,16,96,128]{3,2,1,0:T(8,128)(2,1)} %get-tuple-element.12.pieces_in, f32[1,1024]{1,0:T(1,128)} %get-tuple-element.13.bias_in), custom_call_target="tpu_custom_call" | custom-call | tf_op jit(solution)/shard_map/hand_over/pallas_call | solution.py:776
